TPU v7x, 32 devices: a whole 2x2x4 slice. The times are simulated.
32 devices in a mesh: groups: 2 (over x), expert: 16 (over z, y, core), dp: 1.
Axes of the slice: x: 2, y: 2, z: 4, core: 2. Of those that a mesh axis runs over, the one named last changes fastest.
Arguments:
- latent_pool: bfloat16 [256, 36864], P(('groups', 'expert')), parts along dimension 0, may hold values from -6 to 6
- page_owner: int32 [64, 8], P(('groups', 'expert')), parts along dimension 0, may hold values from 0 to 15, all different within a row; in each aligned block of 2 rows (0 to 1, 2 to 3, ...) at most 2 rows name the same one
- page_slot: int32 [64, 8], P(('groups', 'expert')), parts along dimension 0, may hold values from 0 to 7
- prefix_len: int32 [64], P(('groups', 'expert')), parts along dimension 0, may hold values from 449 to 512
- queries: bfloat16 [64, 32, 36864], P(('groups', 'expert'), None, 'dp'), parts along dimension 0, may hold values from -30 to 30
- new_latent: bfloat16 [64, 18432], P(('groups', 'expert')), parts along dimension 0, may hold values from -5 to 5
- tokens: bfloat16 [2048, 3584], P(('groups', 'expert', 'dp')), parts along dimension 0, may hold values from -6 to 6
- expert_ids: int32 [2048, 4], P(('groups', 'expert', 'dp')), parts along dimension 0, may hold values from 0 to 15, all different within a row; in each aligned block of 64 rows (0 to 63, 64 to 127, ...) at most 24 rows name the same one
- gates: float32 [2048, 4], P(('groups', 'expert', 'dp')), parts along dimension 0, may hold values from 0.2 to 1
- w_gate: bfloat16 [16, 3584, 1024], P(('expert', 'dp')), may hold values from -0.09375 to 0.09375
- w_up: bfloat16 [16, 3584, 1024], P(('expert', 'dp')), may hold values from -0.09375 to 0.09375
- w_down: bfloat16 [16, 1024, 3584], P(('expert', 'dp')), may hold values from -0.1875 to 0.1875
Outputs:
- context: bfloat16 [64, 32, 32768], P(('groups', 'expert'), None, 'dp'), parts along dimension 0
- moe_out: bfloat16 [2048, 3584], P(('groups', 'expert', 'dp')), parts along dimension 0
There are 2 independent parts, one for each index of `groups`. A program takes and returns all parts, laid end to end along the dimension named above; an argument that names none is the same for every part. Nothing has to cross between parts.
Inputs may be any that keep to these rules, and one draw needn't show every extreme that they name: `page_owner`: each row names 8 different owners; within the 2 rows of one device no owner is named more than 2 times, and in some such block one owner is named exactly 2 times. `expert_ids`: each row names 4 different experts; within the 64 rows of one device no expert is named more than 24 times, and in some such block one expert is named exactly 24 times.
All inputs are finite; a program needn't handle non-finite values.
Results may differ from a plain program's by a relative error of at most 0.0057.
Values may be sent and summed in bfloat16 or wider, within the bound.
A program may use at most 128 MiB of HBM per device.

v0:
```python
import jax
import jax.numpy as jnp
from jax import lax
from jax.sharding import PartitionSpec as P

LATENT = 512
ROPE = 64
EXPERTS = 16
CAPP = 2


score_scale = 192.0 ** (-0.5)


def rank_within(labels, groups):
    marks = (labels[:, None] == jnp.arange(groups, dtype=jnp.int32)[None, :]).astype(jnp.int32)
    before = jnp.cumsum(marks, axis=0) - marks
    return jnp.sum(before * marks, axis=1)


def attend_request(packed):
    query_rows, cached, fresh_latent, length = packed
    new_rows = query_rows.shape[0]
    latent_all = LATENT + ROPE
    head_count = query_rows.shape[1] // latent_all
    keys_all = jnp.concatenate([cached, fresh_latent.reshape(new_rows, latent_all)], axis=0)
    query_heads = query_rows.reshape(new_rows, head_count, latent_all)
    scores = (
        jnp.einsum("nhl,kl->hnk", query_heads, keys_all, preferred_element_type=jnp.float32)
        * score_scale
    )
    prefix_cap = cached.shape[0]
    position = jnp.arange(keys_all.shape[0], dtype=jnp.int32)
    row_index = jnp.arange(new_rows, dtype=jnp.int32)
    visible = jnp.where(
        (position < prefix_cap)[None, :],
        (position < length)[None, :],
        (position - prefix_cap)[None, :] <= row_index[:, None],
    )
    scores = jnp.where(visible[None], scores, -1e30)
    highest = jnp.max(scores, axis=-1, keepdims=True)
    weights = jnp.exp(scores - highest)
    probs = (weights / jnp.sum(weights, axis=-1, keepdims=True)).astype(jnp.bfloat16)
    context = jnp.einsum(
        "hnk,kc->nhc", probs, keys_all[:, :LATENT], preferred_element_type=jnp.float32
    )
    return context.reshape(new_rows, head_count * LATENT).astype(jnp.bfloat16)


def expert_mlp(received, w_gate, w_up, w_down):
    features = received.shape[-1]
    flattened = received.reshape(-1, features)
    gate_val = jnp.dot(flattened, w_gate[0], preferred_element_type=jnp.float32)
    upward = jnp.dot(flattened, w_up[0], preferred_element_type=jnp.float32)
    hidden = (jax.nn.silu(gate_val) * upward).astype(jnp.bfloat16)
    part_out = jnp.dot(hidden, w_down[0], preferred_element_type=jnp.float32).astype(jnp.bfloat16)
    return part_out.reshape(received.shape)


def per_device(
    latent_pool,
    page_owner,
    page_slot,
    prefix_len,
    queries,
    new_latent,
    tokens,
    expert_ids,
    gates,
    w_gate,
    w_up,
    w_down,
):
    owner_count = lax.axis_size("expert")
    dp_count = lax.axis_size("dp")
    request_count, page_count = page_owner.shape
    page_rows = latent_pool.shape[1] // (LATENT + ROPE)
    refs_owner = page_owner.reshape(-1)
    slot_index = refs_owner * CAPP + rank_within(refs_owner, owner_count)
    chosen_page = (
        slot_index[:, None] == jnp.arange(owner_count * CAPP, dtype=jnp.int32)[None, :]
    ).astype(jnp.int32)
    asked_slots = jnp.sum(chosen_page * page_slot.reshape(-1)[:, None], axis=0).reshape(
        owner_count, CAPP
    )
    fetched = jnp.take(
        latent_pool,
        lax.all_to_all(asked_slots, "expert", split_axis=0, concat_axis=0, tiled=True),
        axis=0,
    )
    arrived = lax.all_to_all(fetched, "expert", split_axis=0, concat_axis=0, tiled=True)
    pages_flat = arrived.reshape(owner_count * CAPP, -1)
    cached = jnp.take(pages_flat, slot_index, axis=0).reshape(
        request_count, page_count * page_rows, LATENT + ROPE
    )
    context = lax.map(attend_request, (queries, cached, new_latent, prefix_len))
    token_rows, features = tokens.shape
    top_count = expert_ids.shape[1]
    capacity = 3 * token_rows * top_count // (2 * EXPERTS)
    ref_expert = expert_ids.reshape(-1)
    dest_slot = ref_expert * capacity + rank_within(ref_expert, EXPERTS)
    chosen = (
        dest_slot[:, None] == jnp.arange(EXPERTS * capacity, dtype=jnp.int32)[None, :]
    ).astype(jnp.bfloat16)
    repeated = jnp.repeat(tokens, top_count, axis=0)
    buffer = jnp.einsum("re,rd->ed", chosen, repeated, preferred_element_type=jnp.float32).astype(
        jnp.bfloat16
    )
    slice_count = owner_count * dp_count
    split_count = slice_count // EXPERTS
    by_expert = buffer.reshape(EXPERTS, 1, capacity, features)
    outgoing = jnp.broadcast_to(by_expert, (EXPERTS, split_count, capacity, features)).reshape(
        slice_count, capacity, features
    )
    returned = lax.all_to_all(
        expert_mlp(
            lax.all_to_all(outgoing, ("expert", "dp"), split_axis=0, concat_axis=0, tiled=True),
            w_gate,
            w_up,
            w_down,
        ),
        ("expert", "dp"),
        split_axis=0,
        concat_axis=0,
        tiled=True,
    )
    returned = returned.reshape(EXPERTS, split_count, capacity, features)
    summed = jnp.sum(returned, axis=1, dtype=jnp.float32).reshape(EXPERTS * capacity, features)
    weighting = (
        (chosen.astype(jnp.float32) * gates.reshape(-1)[:, None])
        .reshape(token_rows, top_count, -1)
        .sum(axis=1)
    )
    moe_out = jnp.dot(
        weighting, summed, precision=lax.Precision.HIGHEST, preferred_element_type=jnp.float32
    ).astype(jnp.bfloat16)
    return (context, moe_out)


def solution(mesh):
    return jax.shard_map(
        per_device,
        mesh=mesh,
        in_specs=(
            P(("groups", "expert"), None),
            P(("groups", "expert"), None),
            P(("groups", "expert"), None),
            P(("groups", "expert")),
            P(("groups", "expert"), None, "dp"),
            P(("groups", "expert"), None),
            P(("groups", "expert", "dp"), None),
            P(("groups", "expert", "dp"), None),
            P(("groups", "expert", "dp"), None),
            P(("expert", "dp"), None, None),
            P(("expert", "dp"), None, None),
            P(("expert", "dp"), None, None),
        ),
        out_specs=(P(("groups", "expert"), None, "dp"), P(("groups", "expert", "dp"), None)),
        check_vma=False,
    )
```

profile of v0, /device:TPU:15, one launch (start us, length us, event | category | flops | bytes accessed | tf_op | source)
XLA Modules:
  0.0 240.7 jit_solution(10401413183888024273)
XLA Ops:
  2.7 10.2 %all_to_all.30 = s32[16,1,2]{2,1,0:T(1,128)S(1)} all-to-all(s32[16,1,2]{2,1,0:T(1,128)S(1)} %bitcast.93), channel_id=1, replica_groups=mesh['groups'=2,'expert'=16,'dp'=1] {'expert'}, dimensions={0} | all-to-all | bytes 256 | tf_op jit(solution)/shard_map/all_to_all | solution.py:88
  13.2 2.1 gather_fusion
  15.3 2.8 %reshape.256 = bf16[16,2,36864]{2,1,0:T(2,128)(2,1)} reshape(bf16[32,36864]{1,0:T(8,128)(2,1)S(1)} %gather_fusion) | data formatting | bytes 4718592 | tf_op jit(solution)/shard_map/jit(_take)/gather | solution.py:86
  18.1 5.2 %broadcast_select_fusion = bf16[16,2,36864]{2,1,0:T(2,128)(2,1)} fusion(bf16[16,2,36864]{2,1,0:T(2,128)(2,1)} %reshape.256, pred[16,2]{1,0:T(8,128)(4,1)S(1)} %copy.54), kind=kLoop, calls=%fused_computation.41 | loop fusion | flops 1179648 | bytes 4718624 | tf_op jit(solution)/shard_map/jit(_take)/select_n | solution.py:86
  23.3 6.4 %all-to-all-start.1 = ((bf16[16,2,36864]{2,1,0:T(2,128)(2,1)}), bf16[16,2,36864]{2,1,0:T(2,128)(2,1)S(1)}, u32[]{:S(2)}, u32[]{:S(2)}) async-start(bf16[16,2,36864]{2,1,0:T(2,128)(2,1)} %broadcast_select_fusion), calls=%async_computation.1 | async-start | bytes 4718592 | tf_op jit(solution)/shard_map/all_to_all | solution.py:91
  32.6 3.9 %reshape.251 = bf16[256,3584]{1,0:T(8,128)(2,1)} reshape(bf16[64,4,3584]{2,1,0:T(4,128)(2,1)} %broadcast_in_dim.87) | data formatting | bytes 3670016 | tf_op jit(solution)/shard_map/reshape | solution.py:105
  36.6 4.1 %convolution_convert_fusion = bf16[384,3584]{1,0:T(8,128)(2,1)} fusion(bf16[256,3584]{1,0:T(8,128)(2,1)} %reshape.251, s32[256]{0:T(256)S(1)} %multiply_add_fusion.1), kind=kOutput, calls=%fused_computation.39 | convolution fusion | flops 706117632 | bytes 4588544 | tf_op jit(solution)/shard_map/re,rd->ed/dot_general | solution.py:106
  40.6 42.1 %all-to-all-done.1 = bf16[16,2,36864]{2,1,0:T(2,128)(2,1)S(1)} async-done(((bf16[16,2,36864]{2,1,0:T(2,128)(2,1)}), bf16[16,2,36864]{2,1,0:T(2,128)(2,1)S(1)}, u32[]{:S(2)}, u32[]{:S(2)}) %all-to-all-start.1) | async-done | bytes 2359328 | tf_op jit(solution)/shard_map/all_to_all | solution.py:91
  84.2 4.9 %all-to-all-start.2 = ((bf16[16,24,3584]{2,1,0:T(8,128)(2,1)}), bf16[16,24,3584]{2,1,0:T(8,128)(2,1)}, u32[]{:S(2)}, u32[]{:S(2)}) async-start(bf16[16,24,3584]{2,1,0:T(8,128)(2,1)} %bitcast.12), calls=%async_computation.2 | async-start | bytes 5505024 | tf_op jit(solution)/shard_map/all_to_all | solution.py:117
  89.8 2.9 %reshape.249 = bf16[32,36864]{1,0:T(8,128)(2,1)S(1)} reshape(bf16[16,2,36864]{2,1,0:T(2,128)(2,1)} %copy-done.3) | data formatting | bytes 4718592 | tf_op jit(solution)/shard_map/reshape | solution.py:92
  92.7 2.4 gather_fusion.1
  95.0 2.7 %gather.12 = bf16[2,512,576]{2,1,0:T(8,128)(2,1)S(1)} reshape(bf16[16,36864]{1,0:T(8,128)(2,1)} %gather_fusion.1) | data formatting | bytes 2359296 | tf_op jit(solution)/shard_map/jit(_take)/gather | solution.py:93
  99.1 51.5 %all-to-all-done.2 = bf16[16,24,3584]{2,1,0:T(8,128)(2,1)} async-done(((bf16[16,24,3584]{2,1,0:T(8,128)(2,1)}), bf16[16,24,3584]{2,1,0:T(8,128)(2,1)}, u32[]{:S(2)}, u32[]{:S(2)}) %all-to-all-start.2) | async-done | bytes 2752544 | tf_op jit(solution)/shard_map/all_to_all | solution.py:117
  150.6 6.1 %fusion.22 = f32[384,1024]{1,0:T(8,128)S(1)} fusion(bf16[384,3584]{1,0:T(8,128)(2,1)} %bitcast.13, bf16[1,3584,1024]{2,1,0:T(8,128)(2,1)} %param.23), kind=kOutput, calls=%fused_computation.37 | convolution fusion | flops 2818572288 | bytes 11665408 | tf_op jit(solution)/shard_map/dot_general | solution.py:53
  156.7 13.4 %fusion.24 = bf16[384,3584]{1,0:T(8,128)(2,1)} fusion(bf16[1,1024,3584]{2,1,0:T(8,128)(2,1)} %param.25, f32[384,1024]{1,0:T(8,128)S(1)} %fusion.22, bf16[384,3584]{1,0:T(8,128)(2,1)} %bitcast.13, bf16[1,3584,1024]{2,1,0:T(8,128)(2,1)} %param.24), kind=kOutput, calls=%fused_computation.40 | convolution fusion | flops 5640880128 | bytes 21757952 | tf_op jit(solution)/shard_map/dot_general | solution.py:56
  170.1 5.0 %all-to-all-start.3 = ((bf16[16,24,3584]{2,1,0:T(8,128)(2,1)}), bf16[16,24,3584]{2,1,0:T(8,128)(2,1)}, u32[]{:S(2)}, u32[]{:S(2)}) async-start(bf16[16,24,3584]{2,1,0:T(8,128)(2,1)} %bitcast.17), calls=%async_computation.3 | async-start | bytes 5505024 | tf_op jit(solution)/shard_map/all_to_all | solution.py:115
  175.2 55.9 %while.12 = (s32[]{:T(128)}, bf16[2,32,32768]{2,1,0:T(8,128)(2,1)}, bf16[2,512,576]{2,1,0:T(8,128)(2,1)}, bf16[2,18432]{1,0:T(2,128)(2,1)S(1)}, s32[2]{0:T(128)S(1)}, /*index=5*/bf16[2,32,36864]{2,1,0:T(8,128)(2,1)}, s32[]{:T(128)}) while((s32[]{:T(128)}, bf16[2,32,32768]{2,1,0:T(8,128)(2,1)}, bf16[2,512,576]{2,1,0:T(8,128)(2,1)}, ...), condition=%wide.region_6.7_spmd, body=%wide.region_3.6_spmd.sunk | while | flops 2436673536 | bytes 45106180 | solution.py:96
  175.2 2.0 dynamic-slice_bitcast_fusion.2
  177.5 1.8 constant_dynamic-slice_fusion.2
  179.4 4.1 %reshape.278 = bf16[32,64,576]{2,1,0:T(8,128)(2,1)} reshape(bf16[1,32,36864]{2,1,0:T(8,128)(2,1)S(1)} %constant_dynamic-slice_fusion.2) | data formatting | bytes 4718592 | tf_op jit(solution)/shard_map/while/body/eval_jaxpr/reshape | solution.py:27
  183.5 4.5 %fusion.56 = f32[544,32,64]{0,2,1:T(8,128)S(1)} fusion(bf16[32,64,576]{2,1,0:T(8,128)(2,1)} %reshape.278, bf16[32,576]{1,0:T(8,128)(2,1)S(1)} %reshape.279, bf16[512,576]{1,0:T(8,128)(2,1)} %dynamic-slice_bitcast_fusion.2), kind=kOutput, calls=%fused_computation.15.clone.1 | convolution fusion | flops 1284710400 | bytes 7442432 | tf_op jit(solution)/shard_map/while/body/eval_jaxpr/nhl,kl->hnk/dot_general | solution.py:29
  189.2 6.4 %fusion.58 = (f32[64,32]{0,1:T(8,128)S(1)}, f32[64,32,544]{2,0,1:T(8,128)S(1)}) fusion(f32[544,32,64]{0,2,1:T(8,128)S(1)} %fusion.56, pred[32,544]{1,0:T(8,128)(4,1)S(1)} %fusion.57), kind=kOutput, calls=%fused_computation.79.clone.1 | output fusion | flops 6685215 | bytes 8938496 | tf_op jit(solution)/shard_map/while/body/eval_jaxpr/sub | solution.py:42
  195.5 3.3 %convert_bitcast_fusion.2 = bf16[32,64,512]{2,1,0:T(8,128)(2,1)} fusion(f32[64,32,544]{2,0,1:T(8,128)S(1)} %get-tuple-element.139, f32[64,32]{0,1:T(8,128)S(1)} %get-tuple-element.140, bf16[512,576]{1,0:T(8,128)(2,1)S(1)} %copy-done.2, bf16[32,576]{1,0:T(8,128)(2,1)S(1)} %reshape.279), kind=kOutput, calls=%fused_computation.11.clone.1 | convolution fusion | flops 1145241600 | bytes 7188480 | tf_op jit(solution)/shard_map/while/body/eval_jaxpr/hnk,kc->nhc/dot_general | solution.py:44
  198.8 2.9 %convert_element_type.91 = bf16[1,32,32768]{2,1,0:T(8,128)(2,1)S(1)} reshape(bf16[32,64,512]{2,1,0:T(8,128)(2,1)} %convert_bitcast_fusion.2) | data formatting | bytes 4194304 | tf_op jit(solution)/shard_map/while/body/eval_jaxpr/convert_element_type | solution.py:47
  203.1 2.0 dynamic-slice_bitcast_fusion.2
  207.3 4.1 %reshape.278 = bf16[32,64,576]{2,1,0:T(8,128)(2,1)} reshape(bf16[1,32,36864]{2,1,0:T(8,128)(2,1)S(1)} %constant_dynamic-slice_fusion.2) | data formatting | bytes 4718592 | tf_op jit(solution)/shard_map/while/body/eval_jaxpr/reshape | solution.py:27
  211.4 4.5 %fusion.56 = f32[544,32,64]{0,2,1:T(8,128)S(1)} fusion(bf16[32,64,576]{2,1,0:T(8,128)(2,1)} %reshape.278, bf16[32,576]{1,0:T(8,128)(2,1)S(1)} %reshape.279, bf16[512,576]{1,0:T(8,128)(2,1)} %dynamic-slice_bitcast_fusion.2), kind=kOutput, calls=%fused_computation.15.clone.1 | convolution fusion | flops 1284710400 | bytes 7442432 | tf_op jit(solution)/shard_map/while/body/eval_jaxpr/nhl,kl->hnk/dot_general | solution.py:29
  217.1 6.4 %fusion.58 = (f32[64,32]{0,1:T(8,128)S(1)}, f32[64,32,544]{2,0,1:T(8,128)S(1)}) fusion(f32[544,32,64]{0,2,1:T(8,128)S(1)} %fusion.56, pred[32,544]{1,0:T(8,128)(4,1)S(1)} %fusion.57), kind=kOutput, calls=%fused_computation.79.clone.1 | output fusion | flops 6685215 | bytes 8938496 | tf_op jit(solution)/shard_map/while/body/eval_jaxpr/sub | solution.py:42
  223.5 3.3 %convert_bitcast_fusion.2 = bf16[32,64,512]{2,1,0:T(8,128)(2,1)} fusion(f32[64,32,544]{2,0,1:T(8,128)S(1)} %get-tuple-element.139, f32[64,32]{0,1:T(8,128)S(1)} %get-tuple-element.140, bf16[512,576]{1,0:T(8,128)(2,1)S(1)} %copy-done.2, bf16[32,576]{1,0:T(8,128)(2,1)S(1)} %reshape.279), kind=kOutput, calls=%fused_computation.11.clone.1 | convolution fusion | flops 1145241600 | bytes 7188480 | tf_op jit(solution)/shard_map/while/body/eval_jaxpr/hnk,kc->nhc/dot_general | solution.py:44
  226.7 2.9 %convert_element_type.91 = bf16[1,32,32768]{2,1,0:T(8,128)(2,1)S(1)} reshape(bf16[32,64,512]{2,1,0:T(8,128)(2,1)} %convert_bitcast_fusion.2) | data formatting | bytes 4194304 | tf_op jit(solution)/shard_map/while/body/eval_jaxpr/convert_element_type | solution.py:47
  231.1 5.7 %all-to-all-done.3 = bf16[16,24,3584]{2,1,0:T(8,128)(2,1)} async-done(((bf16[16,24,3584]{2,1,0:T(8,128)(2,1)}), bf16[16,24,3584]{2,1,0:T(8,128)(2,1)}, u32[]{:S(2)}, u32[]{:S(2)}) %all-to-all-start.3) | async-done | bytes 2752544 | tf_op jit(solution)/shard_map/all_to_all | solution.py:115
  236.8 4.0 %convolution_convert_fusion.1 = bf16[64,3584]{1,0:T(8,128)(2,1)} fusion(f32[64,384]{1,0:T(8,128)S(1)} %multiply_reduce_fusion, bf16[384,3584]{1,0:T(8,128)(2,1)} %bitcast.18), kind=kOutput, calls=%fused_computation.42 | convolution fusion | flops 1057193984 | bytes 3309568 | tf_op jit(solution)/shard_map/dot_general | solution.py:134
  (77 shorter events, 16.6 us)
Async XLA Ops:
  0.6 12.5 %copy-start = (bf16[8,36864]{1,0:T(8,128)(2,1)S(1)}, bf16[8,36864]{1,0:T(8,128)(2,1)}, u32[]{:S(2)}) copy-start(bf16[8,36864]{1,0:T(8,128)(2,1)} %param.14) | copy-start | bytes 1769476
  23.3 6.4 %copy-start.6 = (s32[64,4]{0,1:T(4,128)S(1)}, s32[64,4]{0,1:T(4,128)}, u32[]{:S(2)}) copy-start(s32[64,4]{0,1:T(4,128)} %param.21) | copy-start | bytes 3076
  23.3 7.5 %copy-start.5 = (bf16[64,3584]{1,0:T(8,128)(2,1)S(1)}, bf16[64,3584]{1,0:T(8,128)(2,1)}, u32[]{:S(2)}) copy-start(bf16[64,3584]{1,0:T(8,128)(2,1)} %param.20) | copy-start | bytes 1376260
  23.3 59.4 %all-to-all-start.1 = ((bf16[16,2,36864]{2,1,0:T(2,128)(2,1)}), bf16[16,2,36864]{2,1,0:T(2,128)(2,1)S(1)}, u32[]{:S(2)}, u32[]{:S(2)}) async-start(bf16[16,2,36864]{2,1,0:T(2,128)(2,1)} %broadcast_select_fusion), calls=%async_computation.1 | async-start | bytes 4718592 | tf_op jit(solution)/shard_map/all_to_all | solution.py:91
  82.8 1.4 copy-start.3
  82.8 6.5 %copy-start.7 = (s32[2,8]{1,0:T(2,128)S(1)}, s32[2,8]{1,0:T(2,128)}, u32[]{:S(2)}) copy-start(s32[2,8]{1,0:T(2,128)} %param.15) | copy-start | bytes 196
  82.8 6.9 %copy-start.8 = (f32[64,4]{0,1:T(4,128)S(1)}, f32[64,4]{0,1:T(4,128)}, u32[]{:S(2)}) copy-start(f32[64,4]{0,1:T(4,128)} %param.22) | copy-start | bytes 3076
  84.2 66.5 %all-to-all-start.2 = ((bf16[16,24,3584]{2,1,0:T(8,128)(2,1)}), bf16[16,24,3584]{2,1,0:T(8,128)(2,1)}, u32[]{:S(2)}, u32[]{:S(2)}) async-start(bf16[16,24,3584]{2,1,0:T(8,128)(2,1)} %bitcast.12), calls=%async_computation.2 | async-start | bytes 5505024 | tf_op jit(solution)/shard_map/all_to_all | solution.py:117
  170.1 5.0 %copy-start.4 = (bf16[2,18432]{1,0:T(2,128)(2,1)S(1)}, bf16[2,18432]{1,0:T(2,128)(2,1)}, u32[]{:S(2)}) copy-start(bf16[2,18432]{1,0:T(2,128)(2,1)} %param.19) | copy-start | bytes 221188
  170.1 5.0 %copy-start.9 = (s32[2]{0:T(128)S(1)}, s32[2]{0:T(128)}, u32[]{:S(2)}) copy-start(s32[2]{0:T(128)} %param.17) | copy-start | bytes 28
  170.1 66.6 %all-to-all-start.3 = ((bf16[16,24,3584]{2,1,0:T(8,128)(2,1)}), bf16[16,24,3584]{2,1,0:T(8,128)(2,1)}, u32[]{:S(2)}, u32[]{:S(2)}) async-start(bf16[16,24,3584]{2,1,0:T(8,128)(2,1)} %bitcast.17), calls=%async_computation.3 | async-start | bytes 5505024 | tf_op jit(solution)/shard_map/all_to_all | solution.py:115
  189.2 6.4 %copy-start.2 = (bf16[512,576]{1,0:T(8,128)(2,1)S(1)}, bf16[512,576]{1,0:T(8,128)(2,1)}, u32[]{:S(2)}) copy-start(bf16[512,576]{1,0:T(8,128)(2,1)} %dynamic-slice_bitcast_fusion.2) | copy-start | bytes 1769476 | tf_op jit(solution)/shard_map/while
  217.1 6.4 %copy-start.2 = (bf16[512,576]{1,0:T(8,128)(2,1)S(1)}, bf16[512,576]{1,0:T(8,128)(2,1)}, u32[]{:S(2)}) copy-start(bf16[512,576]{1,0:T(8,128)(2,1)} %dynamic-slice_bitcast_fusion.2) | copy-start | bytes 1769476 | tf_op jit(solution)/shard_map/while
  231.1 9.7 %copy-start.1 = (bf16[8,36864]{1,0:T(8,128)(2,1)S(1)}, bf16[8,36864]{1,0:T(8,128)(2,1)}, u32[]{:S(2)}) copy-start(bf16[8,36864]{1,0:T(8,128)(2,1)} %param.14) | copy-start | bytes 1769476
where the time goes:
time: 242 us; the launch traced here: 241 us
  waiting for transfers between devices  99.3 us (41%)
  local copies, waits for them, and re-layouts  49.2 us (20%)
  matrix products  43.1 us (18%)
  other arithmetic  21.7 us (9%)
  starting transfers between devices  16.3 us (7%)
  blocking collectives  10.2 us (4%)
    all_to_all x1, waiting for transfers between devices, per_device(): lax.all_to_all(outgoing, ('expert', 'dp'), split_axis=0, concat_axis=0, t...  51.5 us
    all_to_all x1, waiting for transfers between devices, per_device(): lax.all_to_all(fetched, 'expert', split_axis=0, concat_axis=0, tiled=True)  42.1 us
    dot_general x1, matrix products, expert_mlp(): jnp.dot(hidden, w_down[0], preferred_element_type=jnp.float32)  13.4 us
    sub x2, other arithmetic, attend_request(): weights = jnp.exp(scores - highest)  12.7 us
    all_to_all x1, blocking collectives, per_device(): lax.all_to_all(asked_slots, 'expert', split_axis=0, concat_axis=0, tiled=...  10.2 us
    dot_general x2, matrix products, attend_request(): jnp.einsum('nhl,kl->hnk', query_heads, keys_all, preferred_element_type=j...  9 us
    reshape x2, local copies, waits for them, and re-layouts, attend_request(): query_heads = query_rows.reshape(new_rows, head_count, latent_all)  8.28 us
    dot_general x2, matrix products, attend_request(): jnp.einsum('hnk,kc->nhc', probs, keys_all[:, :LATENT], preferred_element_...  6.52 us
  transfers between devices with their start and end apart: 3, of which 3 were waited for; matrix products, arithmetic and copies ran while one was open for 32% of the time, Pallas kernels for 0%

commit v1 on v0

v1 whole, which is shorter than its diff:
```python
import jax
import jax.numpy as jnp
from jax import lax
from jax.experimental import pallas as pl
from jax.experimental.pallas import tpu as pltpu
from jax.sharding import PartitionSpec as P

LATENT = 512
ROPE = 64
LAT = LATENT + ROPE
EXPERTS = 16
WINDOW = 640
LOG2E = 1.4426950408889634
SCALE = 192.0 ** (-0.5)
VMEM_LIMIT = 48 * 1024 * 1024


def attend_kernel(length_ref, q_ref, even_ref, odd_ref, o_ref):
    length = length_ref[pl.program_id(0)]
    new_rows = q_ref.shape[1]
    pairs = q_ref.shape[2] // (2 * LAT)
    values = even_ref[0, :, :LATENT]
    for half, (key_ref, start) in enumerate(((even_ref, 0), (odd_ref, LATENT))):
        rows = jnp.concatenate(
            [q_ref[0, :, p * 2 * LAT + start : p * 2 * LAT + start + WINDOW] for p in range(pairs)],
            axis=0,
        )
        scores = lax.dot_general(
            rows, key_ref[0], (((1,), (1,)), ((), ())), preferred_element_type=jnp.float32
        )
        prefix_cap = scores.shape[1] - new_rows
        position = lax.broadcasted_iota(jnp.int32, scores.shape, 1)
        row = lax.rem(lax.broadcasted_iota(jnp.int32, scores.shape, 0), new_rows)
        visible = jnp.logical_or(
            position < length,
            jnp.logical_and(position >= prefix_cap, position - prefix_cap <= row),
        )
        scores = jnp.where(visible, scores, -1e30)
        highest = jnp.max(scores, axis=-1, keepdims=True)
        weights = jnp.exp2((scores - highest) * (SCALE * LOG2E))
        total = jnp.sum(weights, axis=-1, keepdims=True)
        probs = (weights * (1.0 / total)).astype(jnp.bfloat16)
        context = jnp.dot(probs, values, preferred_element_type=jnp.float32).astype(o_ref.dtype)
        for p in range(pairs):
            at = (2 * p + half) * LATENT
            o_ref[0, :, at : at + LATENT] = context[p * new_rows : (p + 1) * new_rows]


def attend(queries, keys, prefix_len):
    requests, new_rows, width = queries.shape
    heads = width // LAT
    block = 16 if heads % 16 == 0 else 2
    key_rows = keys.shape[1]
    even = jnp.pad(keys, ((0, 0), (0, 0), (0, WINDOW - LAT)))
    odd = jnp.pad(keys, ((0, 0), (0, 0), (WINDOW - LAT, 0)))
    key_spec = pl.BlockSpec((1, key_rows, WINDOW), lambda r, h, *_: (r, 0, 0))
    return pl.pallas_call(
        attend_kernel,
        out_shape=jax.ShapeDtypeStruct((requests, new_rows, heads * LATENT), jnp.bfloat16),
        grid_spec=pltpu.PrefetchScalarGridSpec(
            num_scalar_prefetch=1,
            grid=(requests, heads // block),
            in_specs=[
                pl.BlockSpec((1, new_rows, block * LAT), lambda r, h, *_: (r, 0, h)),
                key_spec,
                key_spec,
            ],
            out_specs=pl.BlockSpec((1, new_rows, block * LATENT), lambda r, h, *_: (r, 0, h)),
        ),
        compiler_params=pltpu.CompilerParams(vmem_limit_bytes=VMEM_LIMIT),
        cost_estimate=pl.CostEstimate(
            flops=2 * requests * new_rows * heads * key_rows * (LAT + LATENT),
            bytes_accessed=2 * requests * new_rows * heads * (LAT + LATENT),
            transcendentals=requests * new_rows * heads * key_rows,
        ),
    )(prefix_len, queries, even, odd)


def mlp_kernel(x_ref, gate_ref, up_ref, down_ref, o_ref, total):
    step = pl.program_id(0)
    x = x_ref[...]
    gate_val = jnp.dot(x, gate_ref[0], preferred_element_type=jnp.float32)
    upward = jnp.dot(x, up_ref[0], preferred_element_type=jnp.float32)
    hidden = (gate_val / (1.0 + jnp.exp(-gate_val)) * upward).astype(jnp.bfloat16)
    columns = 512
    for c in range(0, o_ref.shape[1], columns):
        product = jnp.dot(
            hidden, down_ref[0, :, c : c + columns], preferred_element_type=jnp.float32
        )

        @pl.when(step == 0)
        def _():
            total[:, c : c + columns] = product

        @pl.when(step > 0)
        def _():
            total[:, c : c + columns] += product

    @pl.when(step == pl.num_programs(0) - 1)
    def _():
        o_ref[...] = total[...].astype(o_ref.dtype)


def expert_mlp(x, w_gate, w_up, w_down):
    rows, features = x.shape
    units = w_gate.shape[2]
    tile = min(256, units)
    whole = pl.BlockSpec((rows, features), lambda i: (0, 0), pipeline_mode=pl.Buffered(1))
    return pl.pallas_call(
        mlp_kernel,
        out_shape=jax.ShapeDtypeStruct((rows, features), jnp.bfloat16),
        grid=(units // tile,),
        in_specs=[
            whole,
            pl.BlockSpec((1, features, tile), lambda i: (0, 0, i)),
            pl.BlockSpec((1, features, tile), lambda i: (0, 0, i)),
            pl.BlockSpec((1, tile, features), lambda i: (0, i, 0)),
        ],
        out_specs=pl.BlockSpec((rows, features), lambda i: (0, 0)),
        scratch_shapes=[pltpu.VMEM((rows, features), jnp.float32)],
        compiler_params=pltpu.CompilerParams(vmem_limit_bytes=VMEM_LIMIT),
        cost_estimate=pl.CostEstimate(
            flops=6 * rows * features * units,
            bytes_accessed=6 * features * units + 4 * rows * features,
            transcendentals=rows * units,
        ),
    )(x, w_gate, w_up, w_down)


def per_device(
    latent_pool,
    page_owner,
    page_slot,
    prefix_len,
    queries,
    new_latent,
    tokens,
    expert_ids,
    gates,
    w_gate,
    w_up,
    w_down,
):
    owner_count = lax.axis_size("expert")
    dp_count = lax.axis_size("dp")
    request_count, page_count = page_owner.shape
    pool_rows, page_width = latent_pool.shape
    page_rows = page_width // LAT
    token_rows, features = tokens.shape
    top_count = expert_ids.shape[1]
    capacity = 3 * token_rows * top_count // (2 * EXPERTS)
    slice_count = owner_count * dp_count
    split_count = slice_count // EXPERTS
    both = ("expert", "dp")

    all_ids = lax.all_gather(expert_ids, both, axis=0, tiled=False)
    all_tokens = lax.all_gather(tokens, both, axis=0, tiled=True)
    pool = lax.all_gather(latent_pool, "expert", axis=0, tiled=True)

    mine = (lax.axis_index("expert") * dp_count + lax.axis_index("dp")) // split_count
    named = jnp.any(all_ids == mine, axis=2).astype(jnp.bfloat16)
    earlier = (jnp.arange(token_rows)[:, None] < jnp.arange(token_rows)[None, :]).astype(jnp.bfloat16)
    rank = jnp.dot(named, earlier, preferred_element_type=jnp.float32).astype(jnp.int32)
    place = jnp.arange(slice_count, dtype=jnp.int32)[:, None] * capacity + rank
    place = jnp.where(named > 0, place, -1).reshape(-1)
    dispatch = (
        jnp.arange(slice_count * capacity, dtype=jnp.int32)[:, None] == place[None, :]
    ).astype(jnp.bfloat16)
    received = jnp.dot(dispatch, all_tokens, preferred_element_type=jnp.float32).astype(jnp.bfloat16)
    parts = expert_mlp(received, w_gate, w_up, w_down)
    returned = lax.all_to_all(
        parts.reshape(slice_count, capacity, features), both, split_axis=0, concat_axis=0, tiled=True
    )

    page_at = (page_owner * pool_rows + page_slot).reshape(-1)
    cached = pool.at[page_at].get(mode="promise_in_bounds").reshape(
        request_count, page_count * page_rows, LAT
    )
    keys = jnp.concatenate([cached, new_latent.reshape(request_count, -1, LAT)], axis=1)
    context = attend(queries, keys, prefix_len)

    own_rows = jnp.arange(token_rows * top_count) // top_count
    chosen = (expert_ids.reshape(-1)[:, None] == jnp.arange(EXPERTS)[None, :]).astype(jnp.float32)
    tokens_before = (own_rows[None, :] < own_rows[:, None]).astype(jnp.float32)
    own_rank = jnp.sum(jnp.dot(tokens_before, chosen) * chosen, axis=1).astype(jnp.int32)
    dest = (expert_ids.reshape(-1) * capacity + own_rank).reshape(token_rows, top_count)
    weighting = jnp.sum(
        jnp.where(
            dest[:, :, None] == jnp.arange(EXPERTS * capacity, dtype=jnp.int32)[None, None, :],
            gates[:, :, None],
            0.0,
        ),
        axis=1,
    )
    returned = returned.reshape(EXPERTS, split_count, capacity, features)
    summed = jnp.sum(returned, axis=1, dtype=jnp.float32).reshape(EXPERTS * capacity, features)
    moe_out = jnp.dot(
        weighting, summed, precision=lax.Precision.HIGHEST, preferred_element_type=jnp.float32
    ).astype(jnp.bfloat16)
    return (context, moe_out)


def solution(mesh):
    return jax.shard_map(
        per_device,
        mesh=mesh,
        in_specs=(
            P(("groups", "expert"), None),
            P(("groups", "expert"), None),
            P(("groups", "expert"), None),
            P(("groups", "expert")),
            P(("groups", "expert"), None, "dp"),
            P(("groups", "expert"), None),
            P(("groups", "expert", "dp"), None),
            P(("groups", "expert", "dp"), None),
            P(("groups", "expert", "dp"), None),
            P(("expert", "dp"), None, None),
            P(("expert", "dp"), None, None),
            P(("expert", "dp"), None, None),
        ),
        out_specs=(P(("groups", "expert"), None, "dp"), P(("groups", "expert", "dp"), None)),
        check_vma=False,
    )
```

time: 242 us -> 247 us (1.021)
  the two profiles are of different devices: /device:TPU:15 before, /device:TPU:27 now
where the time goes in v1:
time: 247 us
  waiting for transfers between devices  148 us (60%)
  Pallas kernels  37.2 us (15%)
  blocking collectives  17.8 us (7%)
  local copies, waits for them, and re-layouts  14.7 us (6%)
  between operations  14.2 us (6%)
  matrix products  8.84 us (4%)
  starting transfers between devices  5.99 us (2%)
    all_gather x1, waiting for transfers between devices, per_device(): pool = lax.all_gather(latent_pool, 'expert', axis=0, tiled=True)  95 us
    all_gather x1, waiting for transfers between devices, per_device(): all_tokens = lax.all_gather(tokens, both, axis=0, tiled=True)  51.7 us
    pallas_call x1, Pallas kernels, expert_mlp(): pl.pallas_call(mlp_kernel, out_shape=jax.ShapeDtypeStruct((rows, features...  19.5 us
    all_gather x1, blocking collectives, per_device(): all_ids = lax.all_gather(expert_ids, both, axis=0, tiled=False)  17.8 us
    pallas_call x1, Pallas kernels, attend(): pl.pallas_call(attend_kernel, out_shape=jax.ShapeDtypeStruct((requests, n...  17.7 us
    gather x1, local copies, waits for them, and re-layouts, per_device(): pool.at[page_at].get(mode='promise_in_bounds')  8.27 us
    dot_general x1, matrix products, per_device(): jnp.dot(dispatch, all_tokens, preferred_element_type=jnp.float32)  6.3 us
    all_to_all x1, starting transfers between devices, per_device(): lax.all_to_all(parts.reshape(slice_count, capacity, features), both, spli...  5.91 us
  transfers between devices with their start and end apart: 3, of which 2 were waited for; matrix products, arithmetic and copies ran while one was open for 9% of the time, Pallas kernels for 15%

profile of v1, /device:TPU:27, one launch (start us, length us, event | category | flops | bytes accessed | tf_op | source)
XLA Modules:
  0.0 247.1 jit_solution(6062164366923434030)
XLA Ops:
  7.2 0.0 all-gather.7.cloned.1.call-start
  7.2 0.7 all-gather.7.cloned.1.call-update
  7.9 0.0 all-gather.5.cloned.1.call-start
  7.9 0.7 all-gather.5.cloned.1.call-update
  8.7 17.8 %all-gather.1 = s32[16,64,4]{1,2,0:T(4,128)S(1)} all-gather(s32[1,64,4]{1,2,0:T(4,128)} %bitcast.10), channel_id=2, replica_groups=mesh['groups'=2,'expert'=16,'dp'=1] {'expert','dp'}, dimensions={0}, use_global_device_ids=true | all-gather | bytes 17408 | tf_op jit(solution)/shard_map/all_gather | solution.py:156
  26.5 0.1 fusion.2
  26.6 0.1 eq.59
  26.7 51.7 %all-gather.7.cloned.1.call-done = bf16[1024,3584]{1,0:T(8,128)(2,1)} async-done(((bf16[64,3584]{1,0:T(8,128)(2,1)}), bf16[1024,3584]{1,0:T(8,128)(2,1)}) %all-gather.7.cloned.1.call-update) | async-done | bytes 7340048 | tf_op jit(solution)/shard_map/all_gather | solution.py:157
  78.4 6.3 %convolution_convert_fusion.x_ref = bf16[384,3584]{1,0:T(8,128)(2,1)S(1)} fusion(bf16[1024,3584]{1,0:T(8,128)(2,1)} %all-gather.7.cloned.1.call-done, s32[1024]{0:T(1024)S(1)} %eq.59), kind=kOutput, calls=%fused_computation.1 | convolution fusion | flops 2820341760 | bytes 10096640 | tf_op jit(solution)/shard_map/dot_general | solution.py:169
  84.7 19.5 %shard_map.132 = bf16[384,3584]{1,0:T(8,128)(2,1)} custom-call(bf16[384,3584]{1,0:T(8,128)(2,1)S(1)} %convolution_convert_fusion.x_ref, bf16[1,3584,1024]{2,1,0:T(8,128)(2,1)} %gate_ref.1, bf16[1,3584,1024]{2,1,0:T(8,128)(2,1)} %up_ref.1, bf16[1,1024,3584]{2,1,0:T(8,128)(2,1)} %down_ref.1), custom_call_target="tpu_custom_call" | custom-call | flops 8455716864 | bytes 27525120 | tf_op jit(solution)/shard_map/pallas_call | solution.py:109
  104.2 0.0 copy-start.1
  104.2 0.0 copy-start.3
  104.2 5.9 %all-to-all-start = ((bf16[16,24,3584]{2,1,0:T(8,128)(2,1)}), bf16[16,24,3584]{2,1,0:T(8,128)(2,1)S(1)}, u32[]{:S(2)}, u32[]{:S(2)}) async-start(bf16[16,24,3584]{2,1,0:T(8,128)(2,1)} %bitcast.2), calls=%async_computation | async-start | bytes 5505024 | tf_op jit(solution)/shard_map/all_to_all | solution.py:171
  110.2 0.0 copy-done.2
  110.2 0.1 copy.28
  110.3 0.1 reshape.94
  110.4 0.0 copy-done.1
  110.4 0.1 reshape.96
  110.5 0.1 eq.49
  110.6 0.3 fusion
  110.9 0.1 convert_element_type.30
  111.0 0.1 copy.29
  111.1 0.1 select_reduce_fusion
  111.3 95.0 %all-gather.5.cloned.1.call-done = bf16[128,36864]{1,0:T(8,128)(2,1)} async-done(((bf16[8,36864]{1,0:T(8,128)(2,1)}), bf16[128,36864]{1,0:T(8,128)(2,1)}) %all-gather.5.cloned.1.call-update) | async-done | bytes 9437200 | tf_op jit(solution)/shard_map/all_gather | solution.py:158
  206.2 8.3 %gather_fusion = bf16[16,36864]{1,0:T(8,128)(2,1)} fusion(bf16[128,36864]{1,0:T(8,128)(2,1)} %all-gather.5.cloned.1.call-done, s32[1024]{0:T(1024)S(1)} %pad_clamp_fusion), kind=kCustom, calls=%fused_computation | custom fusion | bytes 2359360 | tf_op jit(solution)/shard_map/gather | solution.py:176
  214.5 3.5 %reshape.95 = bf16[2,512,576]{2,1,0:T(8,128)(2,1)} reshape(bf16[16,36864]{1,0:T(8,128)(2,1)} %gather_fusion) | data formatting | bytes 2359296 | tf_op jit(solution)/shard_map/reshape | solution.py:176
  218.0 1.4 constant_dynamic-update-slice_fusion.1
  219.4 0.0 copy-start
  219.4 0.9 fusion.9
  220.3 17.7 %shard_map.131 = bf16[2,32,32768]{2,1,0:T(8,128)(2,1)} custom-call(s32[2]{0:T(128)S(1)} %copy-done, bf16[2,32,36864]{2,1,0:T(8,128)(2,1)} %q_ref.1, bf16[2,544,640]{2,1,0:T(8,128)(2,1)S(1)} %get-tuple-element.3.even_ref, bf16[2,544,640]{2,1,0:T(8,128)(2,1)S(1)} %get-tuple-element.2.odd_ref), custom_call_target="tpu_custom_call" | custom-call | flops 4848615424 | bytes 8912896 | tf_op jit(solution)/shard_map/pallas_call | solution.py:57
  238.0 0.0 all-to-all-done
  238.0 2.2 convolution_convert_fusion.1
  (16 shorter events, 0.1 us)
Async XLA Ops:
  7.2 71.2 %all-gather.7.cloned.1.call-start = ((), (), s32[]{:S(2)}) async-start(), calls=%async_computation.2 | async-start | bytes 7798784 | tf_op jit(solution)/shard_map/all_gather | solution.py:157
  7.9 198.3 %all-gather.5.cloned.1.call-start = ((), (), s32[]{:S(2)}) async-start(), calls=%async_computation.1 | async-start | bytes 10027008 | tf_op jit(solution)/shard_map/all_gather | solution.py:158
  104.2 5.9 %copy-start.2 = (s32[64,4]{0,1:T(4,128)S(1)}, s32[64,4]{0,1:T(4,128)}, u32[]{:S(2)}) copy-start(s32[64,4]{0,1:T(4,128)} %param.19) | copy-start | bytes 3076
  104.2 6.0 %copy-start.4 = (s32[2,8]{1,0:T(2,128)S(1)}, s32[2,8]{1,0:T(2,128)}, u32[]{:S(2)}) copy-start(s32[2,8]{1,0:T(2,128)} %param.14) | copy-start | bytes 196
  104.2 6.0 %copy-start.5 = (s32[2,8]{1,0:T(2,128)S(1)}, s32[2,8]{1,0:T(2,128)}, u32[]{:S(2)}) copy-start(s32[2,8]{1,0:T(2,128)} %param.13) | copy-start | bytes 196
  104.2 6.1 %copy-start.1 = (bf16[2,18432]{1,0:T(2,128)(2,1)S(1)}, bf16[2,18432]{1,0:T(2,128)(2,1)}, u32[]{:S(2)}) copy-start(bf16[2,18432]{1,0:T(2,128)(2,1)} %param.17) | copy-start | bytes 221188
  104.2 6.9 %copy-start.3 = (f32[64,4]{0,1:T(4,128)S(1)}, f32[64,4]{0,1:T(4,128)}, u32[]{:S(2)}) copy-start(f32[64,4]{0,1:T(4,128)} %param.20) | copy-start | bytes 3076
  104.2 133.8 %all-to-all-start = ((bf16[16,24,3584]{2,1,0:T(8,128)(2,1)}), bf16[16,24,3584]{2,1,0:T(8,128)(2,1)S(1)}, u32[]{:S(2)}, u32[]{:S(2)}) async-start(bf16[16,24,3584]{2,1,0:T(8,128)(2,1)} %bitcast.2), calls=%async_computation | async-start | bytes 5505024 | tf_op jit(solution)/shard_map/all_to_all | solution.py:171
  219.4 0.9 copy-start
Sparse Core Ops, SparseCore 0:
  10.3 68.0 all-gather.6
  80.7 125.4 all-gather.4

commit v2 on v1

--- a/solution.py
+++ b/solution.py
@@ -9,6 +9,8 @@
 ROPE = 64
 LAT = LATENT + ROPE
 EXPERTS = 16
+CAPP = 2
+ASK_LANES = 128
 WINDOW = 640
 LOG2E = 1.4426950408889634
 SCALE = 192.0 ** (-0.5)
@@ -102,7 +104,7 @@
 
 
 def expert_mlp(x, w_gate, w_up, w_down):
-    rows, features = x.shape
+    rows, features = x.shape[0], w_gate.shape[1]
     units = w_gate.shape[2]
     tile = min(256, units)
     whole = pl.BlockSpec((rows, features), lambda i: (0, 0), pipeline_mode=pl.Buffered(1))
@@ -153,49 +155,85 @@
     split_count = slice_count // EXPERTS
     both = ("expert", "dp")
 
-    all_ids = lax.all_gather(expert_ids, both, axis=0, tiled=False)
-    all_tokens = lax.all_gather(tokens, both, axis=0, tiled=True)
-    pool = lax.all_gather(latent_pool, "expert", axis=0, tiled=True)
-
-    mine = (lax.axis_index("expert") * dp_count + lax.axis_index("dp")) // split_count
-    named = jnp.any(all_ids == mine, axis=2).astype(jnp.bfloat16)
-    earlier = (jnp.arange(token_rows)[:, None] < jnp.arange(token_rows)[None, :]).astype(jnp.bfloat16)
-    rank = jnp.dot(named, earlier, preferred_element_type=jnp.float32).astype(jnp.int32)
-    place = jnp.arange(slice_count, dtype=jnp.int32)[:, None] * capacity + rank
-    place = jnp.where(named > 0, place, -1).reshape(-1)
-    dispatch = (
-        jnp.arange(slice_count * capacity, dtype=jnp.int32)[:, None] == place[None, :]
-    ).astype(jnp.bfloat16)
-    received = jnp.dot(dispatch, all_tokens, preferred_element_type=jnp.float32).astype(jnp.bfloat16)
-    parts = expert_mlp(received, w_gate, w_up, w_down)
+    wanted = jnp.any(
+        expert_ids[:, :, None] == jnp.arange(EXPERTS, dtype=jnp.int32)[None, None, :], axis=1
+    ).astype(jnp.bfloat16)
+    before = (
+        jnp.arange(token_rows)[:, None] > jnp.arange(token_rows)[None, :]
+    ).astype(jnp.bfloat16)
+    rank = jnp.dot(before, wanted, preferred_element_type=jnp.float32).astype(jnp.int32)
+    place = jnp.where(
+        wanted > 0, rank + capacity * jnp.arange(EXPERTS, dtype=jnp.int32)[None, :], -1
+    )
+    chosen = place.T[:, None, :] == jnp.arange(EXPERTS * capacity, dtype=jnp.int32).reshape(
+        EXPERTS, capacity, 1
+    )
+    dispatch = chosen.reshape(EXPERTS * capacity, token_rows).astype(jnp.bfloat16)
+    buffer = jnp.dot(dispatch, tokens, preferred_element_type=jnp.float32).astype(jnp.bfloat16)
+
+    refs_owner = page_owner.reshape(-1)
+    named = refs_owner[:, None] == jnp.arange(owner_count, dtype=jnp.int32)[None, :]
+    ref_at = jnp.arange(refs_owner.shape[0], dtype=jnp.int32)
+    same = (refs_owner[:, None] == refs_owner[None, :]) & (ref_at[None, :] < ref_at[:, None])
+    ref_rank = jnp.sum(same.astype(jnp.int32), axis=1)
+    asks = jnp.sum(
+        jnp.where(
+            named[:, :, None]
+            & (ref_rank[:, None, None] == jnp.arange(ASK_LANES, dtype=jnp.int32)[None, None, :]),
+            page_slot.reshape(-1)[:, None, None],
+            0,
+        ),
+        axis=0,
+    ).astype(jnp.bfloat16)
+    asks = jnp.repeat(asks, dp_count, axis=0)
+    outgoing = jnp.broadcast_to(
+        buffer.reshape(EXPERTS, 1, capacity, features), (EXPERTS, split_count, capacity, features)
+    ).reshape(slice_count, capacity, features)
+    outgoing = jnp.concatenate(
+        [outgoing, jnp.broadcast_to(asks[:, None, :], (slice_count, capacity, ASK_LANES))], axis=2
+    )
+    received = lax.all_to_all(outgoing, both, split_axis=0, concat_axis=0, tiled=True)
+
+    asked = received[:, 0, features : features + CAPP].reshape(owner_count, dp_count, CAPP)[:, 0]
+    lines = latent_pool.reshape(pool_rows, page_width // 128, 128)
+    fetched = lines.at[asked.astype(jnp.int32)].get(mode="clip")
+    arrived = lax.all_to_all(fetched, "expert", split_axis=0, concat_axis=0, tiled=True)
+
+    parts = expert_mlp(received.reshape(-1, features + ASK_LANES), w_gate, w_up, w_down)
+    parts, arrived = lax.optimization_barrier((parts, arrived))
     returned = lax.all_to_all(
         parts.reshape(slice_count, capacity, features), both, split_axis=0, concat_axis=0, tiled=True
     )
 
-    page_at = (page_owner * pool_rows + page_slot).reshape(-1)
-    cached = pool.at[page_at].get(mode="promise_in_bounds").reshape(
-        request_count, page_count * page_rows, LAT
+    page_at = refs_owner * CAPP + ref_rank
+    cached = (
+        arrived.reshape(owner_count * CAPP, page_width // 128, 128)
+        .at[page_at]
+        .get(mode="clip")
+        .reshape(request_count, page_count * page_rows, LAT)
     )
     keys = jnp.concatenate([cached, new_latent.reshape(request_count, -1, LAT)], axis=1)
     context = attend(queries, keys, prefix_len)
 
-    own_rows = jnp.arange(token_rows * top_count) // top_count
-    chosen = (expert_ids.reshape(-1)[:, None] == jnp.arange(EXPERTS)[None, :]).astype(jnp.float32)
-    tokens_before = (own_rows[None, :] < own_rows[:, None]).astype(jnp.float32)
-    own_rank = jnp.sum(jnp.dot(tokens_before, chosen) * chosen, axis=1).astype(jnp.int32)
-    dest = (expert_ids.reshape(-1) * capacity + own_rank).reshape(token_rows, top_count)
-    weighting = jnp.sum(
+    summed = returned.reshape(EXPERTS, split_count, capacity, features)
+    summed = jnp.sum(summed, axis=1, dtype=jnp.float32).reshape(EXPERTS * capacity, features)
+    weight = jnp.sum(
         jnp.where(
-            dest[:, :, None] == jnp.arange(EXPERTS * capacity, dtype=jnp.int32)[None, None, :],
+            expert_ids[:, :, None] == jnp.arange(EXPERTS, dtype=jnp.int32)[None, None, :],
             gates[:, :, None],
             0.0,
         ),
         axis=1,
     )
-    returned = returned.reshape(EXPERTS, split_count, capacity, features)
-    summed = jnp.sum(returned, axis=1, dtype=jnp.float32).reshape(EXPERTS * capacity, features)
-    moe_out = jnp.dot(
-        weighting, summed, precision=lax.Precision.HIGHEST, preferred_element_type=jnp.float32
+    weighting = jnp.where(chosen, weight.T[:, None, :], 0.0).reshape(
+        EXPERTS * capacity, token_rows
+    )
+    moe_out = lax.dot_general(
+        weighting,
+        summed,
+        (((0,), (0,)), ((), ())),
+        precision=lax.Precision.HIGHEST,
+        preferred_element_type=jnp.float32,
     ).astype(jnp.bfloat16)
     return (context, moe_out)
 

time: 247 us -> 208 us (0.84)
  the two profiles are of different devices: /device:TPU:27 before, /device:TPU:15 now
where the time goes in v2:
time: 208 us; the launch traced here: 207 us
  waiting for transfers between devices  129 us (62%)
  Pallas kernels  35.7 us (17%)
  local copies, waits for them, and re-layouts  18.2 us (9%)
  starting transfers between devices  16.6 us (8%)
  matrix products  3.32 us (2%)
  other arithmetic  3.13 us (2%)
    all_to_all x1, waiting for transfers between devices, per_device(): lax.all_to_all(outgoing, both, split_axis=0, concat_axis=0, tiled=True)  61.5 us
    all_to_all x1, waiting for transfers between devices, per_device(): lax.all_to_all(parts.reshape(slice_count, capacity, features), both, spli...  34.3 us
    all_to_all x1, waiting for transfers between devices, per_device(): lax.all_to_all(fetched, 'expert', split_axis=0, concat_axis=0, tiled=True)  33.6 us
    pallas_call x1, Pallas kernels, expert_mlp(): pl.pallas_call(mlp_kernel, out_shape=jax.ShapeDtypeStruct((rows, features...  17.9 us
    pallas_call x1, Pallas kernels, attend(): pl.pallas_call(attend_kernel, out_shape=jax.ShapeDtypeStruct((requests, n...  17.8 us
    all_to_all x1, starting transfers between devices, per_device(): lax.all_to_all(outgoing, both, split_axis=0, concat_axis=0, tiled=True)  6.69 us
    unnamed x17, local copies, waits for them, and re-layouts  5.06 us
    all_to_all x1, starting transfers between devices, per_device(): lax.all_to_all(parts.reshape(slice_count, capacity, features), both, spli...  5.04 us
  transfers between devices with their start and end apart: 3, of which 3 were waited for; matrix products, arithmetic and copies ran while one was open for 6% of the time, Pallas kernels for 17%

profile of v2, /device:TPU:15, one launch (start us, length us, event | category | flops | bytes accessed | tf_op | source)
XLA Modules:
  0.0 207.2 jit_solution(16406005316634227044)
XLA Ops:
  0.7 0.8 eq.97
  1.5 0.2 convert_reduce_fusion
  1.7 0.1 iota_compare_fusion.5
  1.7 0.8 broadcast_in_dim.41
  2.6 0.7 fusion.9
  3.3 0.1 select_reduce_fusion
  3.4 0.1 reshape.172
  3.5 0.1 fusion.2
  3.6 0.2 bitcast_compare_fusion
  3.8 0.9 convolution_convert_fusion
  4.6 1.8 pad_maximum_fusion
  6.4 6.7 %all-to-all-start = ((bf16[16,24,3712]{2,1,0:T(8,128)(2,1)}), bf16[16,24,3712]{2,1,0:T(8,128)(2,1)S(1)}, u32[]{:S(2)}, u32[]{:S(2)}) async-start(bf16[16,24,3712]{2,1,0:T(8,128)(2,1)} %pad_maximum_fusion), calls=%async_computation | async-start | bytes 5701632 | tf_op jit(solution)/shard_map/all_to_all | solution.py:195
  13.1 0.1 mul.23
  13.2 2.0 copy.35
  15.2 61.5 %all-to-all-done = bf16[16,24,3712]{2,1,0:T(8,128)(2,1)S(1)} async-done(((bf16[16,24,3712]{2,1,0:T(8,128)(2,1)}), bf16[16,24,3712]{2,1,0:T(8,128)(2,1)S(1)}, u32[]{:S(2)}, u32[]{:S(2)}) %all-to-all-start) | async-done | bytes 2850848 | tf_op jit(solution)/shard_map/all_to_all | solution.py:195
  76.7 0.1 copy.32
  76.8 0.1 copy.31
  76.9 0.1 reshape.182
  77.0 3.3 %gather_fusion = bf16[32,288,128]{2,1,0:T(8,128)(2,1)} fusion(bf16[8,288,128]{2,1,0:T(8,128)(2,1)} %bitcast.35, s32[1024]{0:T(1024)S(1)} %get-tuple-element.9), kind=kCustom, calls=%fused_computation | custom fusion | bytes 4718720 | tf_op jit(solution)/shard_map/gather | solution.py:199
  80.3 4.9 %all-to-all-start.1 = ((bf16[16,2,288,128]{3,2,1,0:T(8,128)(2,1)}), bf16[16,2,288,128]{3,2,1,0:T(8,128)(2,1)}, u32[]{:S(2)}, u32[]{:S(2)}) async-start(bf16[16,2,288,128]{3,2,1,0:T(8,128)(2,1)} %bitcast.37), calls=%async_computation.1 | async-start | bytes 4718592 | tf_op jit(solution)/shard_map/all_to_all | solution.py:200
  85.2 17.9 %shard_map.131 = bf16[384,3584]{1,0:T(8,128)(2,1)S(1)} custom-call(bf16[384,3712]{1,0:T(8,128)(2,1)S(1)} %bitcast.33, bf16[1,3584,1024]{2,1,0:T(8,128)(2,1)} %gate_ref.1, bf16[1,3584,1024]{2,1,0:T(8,128)(2,1)} %up_ref.1, bf16[1,1024,3584]{2,1,0:T(8,128)(2,1)} %down_ref.1), custom_call_target="tpu_custom_call" | custom-call | flops 8455716864 | bytes 27525120 | tf_op jit(solution)/shard_map/pallas_call | solution.py:111
  103.2 1.5 copy-done.1
  104.7 33.6 %all-to-all-done.1 = bf16[16,2,288,128]{3,2,1,0:T(8,128)(2,1)} async-done(((bf16[16,2,288,128]{3,2,1,0:T(8,128)(2,1)}), bf16[16,2,288,128]{3,2,1,0:T(8,128)(2,1)}, u32[]{:S(2)}, u32[]{:S(2)}) %all-to-all-start.1) | async-done | bytes 2359328 | tf_op jit(solution)/shard_map/all_to_all | solution.py:200
  138.4 5.0 %all-to-all-start.2 = ((bf16[16,24,3584]{2,1,0:T(8,128)(2,1)}), bf16[16,24,3584]{2,1,0:T(8,128)(2,1)S(1)}, u32[]{:S(2)}, u32[]{:S(2)}) async-start(bf16[16,24,3584]{2,1,0:T(8,128)(2,1)} %bitcast.34), calls=%async_computation.2 | async-start | bytes 5505024 | tf_op jit(solution)/shard_map/all_to_all | solution.py:204
  143.4 0.1 reshape.177
  143.6 3.4 %gather_fusion.1 = bf16[16,288,128]{2,1,0:T(8,128)(2,1)} fusion(bf16[32,288,128]{2,1,0:T(8,128)(2,1)} %bitcast.7, s32[1024]{0:T(1024)S(1)} %get-tuple-element.8), kind=kCustom, calls=%fused_computation.1 | custom fusion | bytes 2359360 | tf_op jit(solution)/shard_map/gather | solution.py:212
  147.0 3.5 %reshape.176 = bf16[2,512,576]{2,1,0:T(8,128)(2,1)} reshape(bf16[16,288,128]{2,1,0:T(8,128)(2,1)} %gather_fusion.1) | data formatting | bytes 2359296 | tf_op jit(solution)/shard_map/reshape | solution.py:213
  150.5 1.4 constant_dynamic-update-slice_fusion.1
  151.9 0.9 fusion.13
  152.8 17.8 %shard_map.132 = bf16[2,32,32768]{2,1,0:T(8,128)(2,1)} custom-call(s32[2]{0:T(128)S(1)} %copy-done.2, bf16[2,32,36864]{2,1,0:T(8,128)(2,1)} %q_ref.1, bf16[2,544,640]{2,1,0:T(8,128)(2,1)S(1)} %get-tuple-element.7.even_ref, bf16[2,544,640]{2,1,0:T(8,128)(2,1)S(1)} %get-tuple-element.6.odd_ref), custom_call_target="tpu_custom_call" | custom-call | flops 4848615424 | bytes 8912896 | tf_op jit(solution)/shard_map/pallas_call | solution.py:59
  170.6 34.3 %all-to-all-done.2 = bf16[16,24,3584]{2,1,0:T(8,128)(2,1)S(1)} async-done(((bf16[16,24,3584]{2,1,0:T(8,128)(2,1)}), bf16[16,24,3584]{2,1,0:T(8,128)(2,1)S(1)}, u32[]{:S(2)}, u32[]{:S(2)}) %all-to-all-start.2) | async-done | bytes 2752544 | tf_op jit(solution)/shard_map/all_to_all | solution.py:204
  204.9 2.4 %fusion = bf16[64,3584]{1,0:T(8,128)(2,1)} fusion(bf16[16,24,3584]{2,1,0:T(8,128)(2,1)S(1)} %all-to-all-done.2, f32[16,64]{1,0:T(8,128)S(1)} %bitcast.39, s32[16,24]{1,0:T(8,128)S(1)} %multiply_add_fusion, s32[16,64]{1,0:T(8,128)S(1)} %fusion.2), kind=kOutput, calls=%fused_computation.4 | convolution fusion | flops 1057243136 | bytes 3220992 | tf_op jit(solution)/shard_map/dot_general | solution.py:231
  (25 shorter events, 0.2 us)
Async XLA Ops:
  0.6 3.1 %copy-start = (bf16[64,3584]{1,0:T(8,128)(2,1)S(1)}, bf16[64,3584]{1,0:T(8,128)(2,1)}, u32[]{:S(2)}) copy-start(bf16[64,3584]{1,0:T(8,128)(2,1)} %param.18) | copy-start | bytes 1376260
  6.4 6.7 %copy-start.6 = (s32[2,8]{1,0:T(2,128)S(1)}, s32[2,8]{1,0:T(2,128)}, u32[]{:S(2)}) copy-start(s32[2,8]{1,0:T(2,128)} %param.13) | copy-start | bytes 196
  6.4 70.3 %all-to-all-start = ((bf16[16,24,3712]{2,1,0:T(8,128)(2,1)}), bf16[16,24,3712]{2,1,0:T(8,128)(2,1)S(1)}, u32[]{:S(2)}, u32[]{:S(2)}) async-start(bf16[16,24,3712]{2,1,0:T(8,128)(2,1)} %pad_maximum_fusion), calls=%async_computation | async-start | bytes 5701632 | tf_op jit(solution)/shard_map/all_to_all | solution.py:195
  80.3 58.0 %all-to-all-start.1 = ((bf16[16,2,288,128]{3,2,1,0:T(8,128)(2,1)}), bf16[16,2,288,128]{3,2,1,0:T(8,128)(2,1)}, u32[]{:S(2)}, u32[]{:S(2)}) async-start(bf16[16,2,288,128]{3,2,1,0:T(8,128)(2,1)} %bitcast.37), calls=%async_computation.1 | async-start | bytes 4718592 | tf_op jit(solution)/shard_map/all_to_all | solution.py:200
  103.1 1.6 copy-start.1
  138.3 5.0 %copy-start.3 = (bf16[2,18432]{1,0:T(2,128)(2,1)S(1)}, bf16[2,18432]{1,0:T(2,128)(2,1)}, u32[]{:S(2)}) copy-start(bf16[2,18432]{1,0:T(2,128)(2,1)} %param.17) | copy-start | bytes 221188
  138.3 5.2 %copy-start.4 = (s32[64,4]{0,1:T(4,128)S(1)}, s32[64,4]{0,1:T(4,128)}, u32[]{:S(2)}) copy-start(s32[64,4]{0,1:T(4,128)} %param.19) | copy-start | bytes 3076
  138.3 5.2 %copy-start.5 = (f32[64,4]{0,1:T(4,128)S(1)}, f32[64,4]{0,1:T(4,128)}, u32[]{:S(2)}) copy-start(f32[64,4]{0,1:T(4,128)} %param.20) | copy-start | bytes 3076
  138.4 66.5 %all-to-all-start.2 = ((bf16[16,24,3584]{2,1,0:T(8,128)(2,1)}), bf16[16,24,3584]{2,1,0:T(8,128)(2,1)S(1)}, u32[]{:S(2)}, u32[]{:S(2)}) async-start(bf16[16,24,3584]{2,1,0:T(8,128)(2,1)} %bitcast.34), calls=%async_computation.2 | async-start | bytes 5505024 | tf_op jit(solution)/shard_map/all_to_all | solution.py:204
  151.9 0.9 copy-start.2

commit v3 on v2

--- a/solution.py
+++ b/solution.py
@@ -1,3 +1,5 @@
+import functools
+
 import jax
 import jax.numpy as jnp
 from jax import lax
@@ -127,6 +129,95 @@
             transcendentals=rows * units,
         ),
     )(x, w_gate, w_up, w_down)
+
+
+def gather_kernel(n, dp_count, own_ref, all_ref, local_sem, ring_out, ring_in, pair_out, pair_in):
+    flat = lax.axis_index("expert") * dp_count + lax.axis_index("dp")
+    group = lax.axis_index("groups")
+    chip, core = lax.div(flat, 2), lax.rem(flat, 2)
+    if dp_count == 1:
+        column, level = lax.rem(chip, 2), lax.div(chip, 2)
+        place = level + column * (n - 1 - 2 * level)
+    else:
+        place = chip
+
+    def at(offset):
+        q = lax.rem(place + offset + n, n)
+        if dp_count == 1:
+            down = lax.div(q, n // 2)
+            q = 2 * (q + down * (n - 1 - 2 * q)) + down
+        return 2 * q + core
+
+    def copy(src, block, send, recv, target):
+        return pltpu.make_async_remote_copy(
+            src_ref=src,
+            dst_ref=all_ref.at[block],
+            send_sem=send,
+            recv_sem=recv,
+            device_id=(group, lax.div(target, dp_count), lax.rem(target, dp_count)),
+            device_id_type=pl.DeviceIdType.MESH,
+        )
+
+    right, left, other = at(1), at(-1), flat + 1 - 2 * core
+    barrier = pltpu.get_barrier_semaphore()
+    for target in (right, left, other):
+        pl.semaphore_signal(
+            barrier,
+            inc=1,
+            device_id=(group, lax.div(target, dp_count), lax.rem(target, dp_count)),
+            device_id_type=pl.DeviceIdType.MESH,
+        )
+    pl.semaphore_wait(barrier, 3)
+
+    hops = (n // 2, n - 1 - n // 2)
+    ring, pair = {}, []
+
+    def ring_start(way, hop, src, block):
+        k = hop + way * hops[0]
+        ring[way, hop] = copy(src, block, ring_out.at[k], ring_in.at[k], (right, left)[way])
+        ring[way, hop].start()
+
+    def pair_start(src, block):
+        j = len(pair)
+        pair.append(copy(src, block, pair_out.at[j], pair_in.at[j], other))
+        pair[-1].start()
+
+    ring_start(0, 0, own_ref, flat)
+    ring_start(1, 0, own_ref, flat)
+    local = pltpu.make_async_copy(own_ref, all_ref.at[flat], local_sem)
+    local.start()
+    pair_start(own_ref, flat)
+    for hop in range(hops[0]):
+        for way in (0, 1):
+            if hop < hops[way]:
+                block = at((-1, 1)[way] * (hop + 1))
+                ring[way, hop].wait_recv()
+                if hop + 1 < hops[way]:
+                    ring_start(way, hop + 1, all_ref.at[block], block)
+                pair_start(all_ref.at[block], block)
+    for sent in ring.values():
+        sent.wait_send()
+    for sent in pair:
+        sent.wait()
+    local.wait()
+
+
+def gather_all(block, dp_count, count):
+    n = count // 2
+    return pl.pallas_call(
+        functools.partial(gather_kernel, n, dp_count),
+        out_shape=jax.ShapeDtypeStruct((count,) + block.shape, block.dtype),
+        in_specs=[pl.BlockSpec(memory_space=pl.ANY)],
+        out_specs=pl.BlockSpec(memory_space=pl.ANY),
+        scratch_shapes=[
+            pltpu.SemaphoreType.DMA,
+            pltpu.SemaphoreType.DMA((n - 1,)),
+            pltpu.SemaphoreType.DMA((n - 1,)),
+            pltpu.SemaphoreType.DMA((n,)),
+            pltpu.SemaphoreType.DMA((n,)),
+        ],
+        compiler_params=pltpu.CompilerParams(collective_id=0, has_side_effects=True),
+    )(block)
 
 
 def per_device(
@@ -168,8 +259,6 @@
     chosen = place.T[:, None, :] == jnp.arange(EXPERTS * capacity, dtype=jnp.int32).reshape(
         EXPERTS, capacity, 1
     )
-    dispatch = chosen.reshape(EXPERTS * capacity, token_rows).astype(jnp.bfloat16)
-    buffer = jnp.dot(dispatch, tokens, preferred_element_type=jnp.float32).astype(jnp.bfloat16)
 
     refs_owner = page_owner.reshape(-1)
     named = refs_owner[:, None] == jnp.arange(owner_count, dtype=jnp.int32)[None, :]
@@ -179,27 +268,47 @@
     asks = jnp.sum(
         jnp.where(
             named[:, :, None]
-            & (ref_rank[:, None, None] == jnp.arange(ASK_LANES, dtype=jnp.int32)[None, None, :]),
+            & (ref_rank[:, None, None] == jnp.arange(CAPP, dtype=jnp.int32)[None, None, :]),
             page_slot.reshape(-1)[:, None, None],
             0,
         ),
         axis=0,
     ).astype(jnp.bfloat16)
-    asks = jnp.repeat(asks, dp_count, axis=0)
-    outgoing = jnp.broadcast_to(
-        buffer.reshape(EXPERTS, 1, capacity, features), (EXPERTS, split_count, capacity, features)
-    ).reshape(slice_count, capacity, features)
-    outgoing = jnp.concatenate(
-        [outgoing, jnp.broadcast_to(asks[:, None, :], (slice_count, capacity, ASK_LANES))], axis=2
-    )
-    received = lax.all_to_all(outgoing, both, split_axis=0, concat_axis=0, tiled=True)
-
-    asked = received[:, 0, features : features + CAPP].reshape(owner_count, dp_count, CAPP)[:, 0]
+    extra = jnp.concatenate(
+        [
+            expert_ids.astype(jnp.bfloat16),
+            jnp.broadcast_to(asks.reshape(1, -1), (token_rows, owner_count * CAPP)),
+        ],
+        axis=1,
+    )
+    extra = jnp.pad(extra, ((0, 0), (0, ASK_LANES - extra.shape[1])))
+    gathered = gather_all(jnp.concatenate([tokens, extra], axis=1), dp_count, slice_count)
+
+    me = lax.axis_index("expert")
+    first = gathered[:, 0, features:].reshape(owner_count, dp_count, ASK_LANES)[:, 0]
+    asked = first[:, top_count : top_count + owner_count * CAPP]
+    asked = lax.dynamic_index_in_dim(
+        asked.reshape(owner_count, owner_count, CAPP), me, axis=1, keepdims=False
+    )
+
+    mine = ((me * dp_count + lax.axis_index("dp")) // split_count).astype(jnp.bfloat16)
+    routed = jnp.any(gathered[:, :, features : features + top_count] == mine, axis=2)
+    rank_in = jnp.dot(
+        routed.astype(jnp.bfloat16), before.T, preferred_element_type=jnp.float32
+    ).astype(jnp.int32)
+    place_in = jnp.arange(slice_count, dtype=jnp.int32)[:, None] * capacity + rank_in
+    place_in = jnp.where(routed, place_in, -1).reshape(-1)
+    dispatch = (
+        jnp.arange(slice_count * capacity, dtype=jnp.int32)[:, None] == place_in[None, :]
+    ).astype(jnp.bfloat16)
     lines = latent_pool.reshape(pool_rows, page_width // 128, 128)
     fetched = lines.at[asked.astype(jnp.int32)].get(mode="clip")
     arrived = lax.all_to_all(fetched, "expert", split_axis=0, concat_axis=0, tiled=True)
 
-    parts = expert_mlp(received.reshape(-1, features + ASK_LANES), w_gate, w_up, w_down)
+    received = jnp.dot(
+        dispatch, gathered.reshape(slice_count * token_rows, -1), preferred_element_type=jnp.float32
+    ).astype(jnp.bfloat16)
+    parts = expert_mlp(received, w_gate, w_up, w_down)
     parts, arrived = lax.optimization_barrier((parts, arrived))
     returned = lax.all_to_all(
         parts.reshape(slice_count, capacity, features), both, split_axis=0, concat_axis=0, tiled=True

time: 208 us -> 189 us (0.909)
  waiting for transfers between devices: 129 us -> 59.5 us
  Pallas kernels: 35.7 us -> 86.1 us
  matrix products: 3.32 us -> 9.2 us
  starting transfers between devices: 16.6 us -> 11.1 us
    all_to_all x1 -> x0, waiting for transfers between devices: 61.5 us -> none  [per_device(): lax.all_to_all(outgoing, both, split_axis=0, concat_axis=0, tiled=True)]
    pallas_call x0 -> x1, Pallas kernels: none -> 48.9 us  [gather_all(): pl.pallas_call(functools.partial(gather_kernel, n, dp_count), out_shape=j...]
    all_to_all x1, waiting for transfers between devices: 33.6 us -> 25.4 us  [per_device(): lax.all_to_all(fetched, 'expert', split_axis=0, concat_axis=0, tiled=True)]
    all_to_all x1 -> x0, starting transfers between devices: 6.69 us -> none  [per_device(): lax.all_to_all(outgoing, both, split_axis=0, concat_axis=0, tiled=True)]
    dot_general x1 -> x2, matrix products: 0.85 us -> 6.73 us  [the longest x1 6.65 us: per_device(): jnp.dot(dispatch, gathered.reshape(slice_count * token_rows, -1), preferr...]
    unnamed x17 -> x15, local copies, waits for them, and re-layouts: 5.06 us -> 2.93 us
  transfers between devices with their start and end apart: 3 -> 2, of which waited for: 3 -> 2; matrix products, arithmetic and copies ran while one was open for 6% -> 9% of each run, Pallas kernels for 17% -> 20%
where the time goes in v3:
time: 189 us; the launch traced here: 188 us
  Pallas kernels  86.1 us (46%)
  waiting for transfers between devices  59.5 us (31%)
  local copies, waits for them, and re-layouts  16.3 us (9%)
  starting transfers between devices  11.1 us (6%)
  matrix products  9.2 us (5%)
  other arithmetic  4.93 us (3%)
    pallas_call x1, Pallas kernels, gather_all(): pl.pallas_call(functools.partial(gather_kernel, n, dp_count), out_shape=j...  48.9 us
    all_to_all x1, waiting for transfers between devices, per_device(): lax.all_to_all(parts.reshape(slice_count, capacity, features), both, spli...  34.1 us
    all_to_all x1, waiting for transfers between devices, per_device(): lax.all_to_all(fetched, 'expert', split_axis=0, concat_axis=0, tiled=True)  25.4 us
    pallas_call x1, Pallas kernels, expert_mlp(): pl.pallas_call(mlp_kernel, out_shape=jax.ShapeDtypeStruct((rows, features...  19.5 us
    pallas_call x1, Pallas kernels, attend(): pl.pallas_call(attend_kernel, out_shape=jax.ShapeDtypeStruct((requests, n...  17.8 us
    dot_general x1, matrix products, per_device(): jnp.dot(dispatch, gathered.reshape(slice_count * token_rows, -1), preferr...  6.65 us
    all_to_all x1, starting transfers between devices, per_device(): lax.all_to_all(fetched, 'expert', split_axis=0, concat_axis=0, tiled=True)  6.19 us
    all_to_all x1, starting transfers between devices, per_device(): lax.all_to_all(parts.reshape(slice_count, capacity, features), both, spli...  4.88 us
  transfers between devices with their start and end apart: 2, of which 2 were waited for; matrix products, arithmetic and copies ran while one was open for 9% of the time, Pallas kernels for 20%

profile of v3, /device:TPU:15, one launch (start us, length us, event | category | flops | bytes accessed | tf_op | source)
XLA Modules:
  0.0 188.0 jit_solution(12201775328019746429)
XLA Ops:
  0.6 0.8 eq.105
  1.4 0.2 convert_reduce_fusion
  1.7 0.7 broadcast_multiply_fusion
  2.3 0.8 broadcast_in_dim.42
  3.1 0.1 select_reduce_fusion.1
  3.2 0.1 copy.24
  3.3 0.1 reshape.196
  3.4 0.7 convert_element_type.60
  4.1 0.1 copy.25
  4.3 1.8 fusion.7.own_ref
  6.1 48.9 %shard_map.131 = bf16[16,64,3712]{2,1,0:T(8,128)(2,1)} custom-call(bf16[64,3712]{1,0:T(8,128)(2,1)} %fusion.7.own_ref), custom_call_target="tpu_custom_call" | custom-call | tf_op jit(solution)/shard_map/pallas_call | solution.py:207
  55.0 0.8 slice.10
  55.8 0.1 copy.26
  56.0 0.1 reshape.180
  56.3 2.3 %gather_fusion = bf16[32,288,128]{2,1,0:T(8,128)(2,1)} fusion(bf16[8,288,128]{2,1,0:T(8,128)(2,1)S(1)} %bitcast.34, s32[1024]{0:T(1024)S(1)} %get-tuple-element.9), kind=kCustom, calls=%fused_computation | custom fusion | bytes 4718720 | tf_op jit(solution)/shard_map/gather | solution.py:305
  58.6 6.2 %all-to-all-start = ((bf16[16,2,288,128]{3,2,1,0:T(8,128)(2,1)}), bf16[16,2,288,128]{3,2,1,0:T(8,128)(2,1)S(1)}, u32[]{:S(2)}, u32[]{:S(2)}) async-start(bf16[16,2,288,128]{3,2,1,0:T(8,128)(2,1)} %bitcast.4), calls=%async_computation | async-start | bytes 4718592 | tf_op jit(solution)/shard_map/all_to_all | solution.py:306
  64.8 1.3 compare_reduce_fusion
  66.1 0.1 fusion.4
  66.2 6.6 %convolution_convert_fusion.x_ref = bf16[384,3712]{1,0:T(8,128)(2,1)S(1)} fusion(bf16[1024,3712]{1,0:T(8,128)(2,1)} %bitcast.35, s32[1024]{0:T(1024)S(1)} %eq.117), kind=kOutput, calls=%fused_computation.2 | convolution fusion | flops 2921054208 | bytes 10457088 | tf_op jit(solution)/shard_map/dot_general | solution.py:308
  72.9 19.5 %shard_map.132 = bf16[384,3584]{1,0:T(8,128)(2,1)} custom-call(bf16[384,3712]{1,0:T(8,128)(2,1)S(1)} %convolution_convert_fusion.x_ref, bf16[1,3584,1024]{2,1,0:T(8,128)(2,1)} %gate_ref.1, bf16[1,3584,1024]{2,1,0:T(8,128)(2,1)} %up_ref.1, bf16[1,1024,3584]{2,1,0:T(8,128)(2,1)} %down_ref.1), custom_call_target="tpu_custom_call" | custom-call | flops 8455716864 | bytes 27525120 | tf_op jit(solution)/shard_map/pallas_call | solution.py:113
  92.4 25.4 %all-to-all-done = bf16[16,2,288,128]{3,2,1,0:T(8,128)(2,1)S(1)} async-done(((bf16[16,2,288,128]{3,2,1,0:T(8,128)(2,1)}), bf16[16,2,288,128]{3,2,1,0:T(8,128)(2,1)S(1)}, u32[]{:S(2)}, u32[]{:S(2)}) %all-to-all-start) | async-done | bytes 2359328 | tf_op jit(solution)/shard_map/all_to_all | solution.py:306
  117.8 1.4 copy-done.1
  119.2 4.9 %all-to-all-start.1 = ((bf16[16,24,3584]{2,1,0:T(8,128)(2,1)}), bf16[16,24,3584]{2,1,0:T(8,128)(2,1)S(1)}, u32[]{:S(2)}, u32[]{:S(2)}) async-start(bf16[16,24,3584]{2,1,0:T(8,128)(2,1)} %bitcast.10), calls=%async_computation.1 | async-start | bytes 5505024 | tf_op jit(solution)/shard_map/all_to_all | solution.py:313
  124.1 0.1 reshape.172
  124.3 0.1 fusion.2
  124.4 3.5 %gather_fusion.1 = bf16[16,288,128]{2,1,0:T(8,128)(2,1)} fusion(bf16[32,288,128]{2,1,0:T(8,128)(2,1)} %bitcast.36, s32[1024]{0:T(1024)S(1)} %get-tuple-element.8), kind=kCustom, calls=%fused_computation.1 | custom fusion | bytes 2359360 | tf_op jit(solution)/shard_map/gather | solution.py:321
  127.9 3.5 %reshape.171 = bf16[2,512,576]{2,1,0:T(8,128)(2,1)} reshape(bf16[16,288,128]{2,1,0:T(8,128)(2,1)} %gather_fusion.1) | data formatting | bytes 2359296 | tf_op jit(solution)/shard_map/reshape | solution.py:322
  131.4 1.4 constant_dynamic-update-slice_fusion.1
  132.8 0.9 fusion.18
  133.7 17.8 %shard_map.133 = bf16[2,32,32768]{2,1,0:T(8,128)(2,1)} custom-call(s32[2]{0:T(128)S(1)} %copy-done, bf16[2,32,36864]{2,1,0:T(8,128)(2,1)} %q_ref.1, bf16[2,544,640]{2,1,0:T(8,128)(2,1)S(1)} %get-tuple-element.7.even_ref, bf16[2,544,640]{2,1,0:T(8,128)(2,1)S(1)} %get-tuple-element.6.odd_ref), custom_call_target="tpu_custom_call" | custom-call | flops 4848615424 | bytes 8912896 | tf_op jit(solution)/shard_map/pallas_call | solution.py:61
  151.5 34.1 %all-to-all-done.1 = bf16[16,24,3584]{2,1,0:T(8,128)(2,1)S(1)} async-done(((bf16[16,24,3584]{2,1,0:T(8,128)(2,1)}), bf16[16,24,3584]{2,1,0:T(8,128)(2,1)S(1)}, u32[]{:S(2)}, u32[]{:S(2)}) %all-to-all-start.1) | async-done | bytes 2752544 | tf_op jit(solution)/shard_map/all_to_all | solution.py:313
  185.6 2.4 %fusion = bf16[64,3584]{1,0:T(8,128)(2,1)} fusion(bf16[16,24,3584]{2,1,0:T(8,128)(2,1)S(1)} %all-to-all-done.1, f32[16,64]{1,0:T(8,128)S(1)} %bitcast.38, s32[16,24]{1,0:T(8,128)S(1)} %multiply_add_fusion, s32[16,64]{1,0:T(8,128)S(1)} %fusion.2), kind=kOutput, calls=%fused_computation.4 | convolution fusion | flops 1057243136 | bytes 3220992 | tf_op jit(solution)/shard_map/dot_general | solution.py:340
  (30 shorter events, 0.7 us)
Async XLA Ops:
  6.1 50.1 %copy-start.2 = (bf16[8,36864]{1,0:T(8,128)(2,1)S(1)}, bf16[8,36864]{1,0:T(8,128)(2,1)}, u32[]{:S(2)}) copy-start(bf16[8,36864]{1,0:T(8,128)(2,1)} %param.12) | copy-start | bytes 1769476
  58.6 59.2 %all-to-all-start = ((bf16[16,2,288,128]{3,2,1,0:T(8,128)(2,1)}), bf16[16,2,288,128]{3,2,1,0:T(8,128)(2,1)S(1)}, u32[]{:S(2)}, u32[]{:S(2)}) async-start(bf16[16,2,288,128]{3,2,1,0:T(8,128)(2,1)} %bitcast.4), calls=%async_computation | async-start | bytes 4718592 | tf_op jit(solution)/shard_map/all_to_all | solution.py:306
  117.8 1.4 copy-start.1
  117.8 6.3 %copy-start.3 = (bf16[2,18432]{1,0:T(2,128)(2,1)S(1)}, bf16[2,18432]{1,0:T(2,128)(2,1)}, u32[]{:S(2)}) copy-start(bf16[2,18432]{1,0:T(2,128)(2,1)} %param.17) | copy-start | bytes 221188
  117.8 6.4 %copy-start.4 = (s32[64,4]{0,1:T(4,128)S(1)}, s32[64,4]{0,1:T(4,128)}, u32[]{:S(2)}) copy-start(s32[64,4]{0,1:T(4,128)} %param.19) | copy-start | bytes 3076
  117.8 6.5 %copy-start.5 = (f32[64,4]{0,1:T(4,128)S(1)}, f32[64,4]{0,1:T(4,128)}, u32[]{:S(2)}) copy-start(f32[64,4]{0,1:T(4,128)} %param.20) | copy-start | bytes 3076
  119.2 66.3 %all-to-all-start.1 = ((bf16[16,24,3584]{2,1,0:T(8,128)(2,1)}), bf16[16,24,3584]{2,1,0:T(8,128)(2,1)S(1)}, u32[]{:S(2)}, u32[]{:S(2)}) async-start(bf16[16,24,3584]{2,1,0:T(8,128)(2,1)} %bitcast.10), calls=%async_computation.1 | async-start | bytes 5505024 | tf_op jit(solution)/shard_map/all_to_all | solution.py:313
  132.8 0.9 copy-start

commit v4 on v3

--- a/solution.py
+++ b/solution.py
@@ -13,6 +13,7 @@
 EXPERTS = 16
 CAPP = 2
 ASK_LANES = 128
+CHUNKS = 2
 WINDOW = 640
 LOG2E = 1.4426950408889634
 SCALE = 192.0 ** (-0.5)
@@ -148,10 +149,15 @@
             q = 2 * (q + down * (n - 1 - 2 * q)) + down
         return 2 * q + core
 
-    def copy(src, block, send, recv, target):
+    rows = own_ref.shape[0] // CHUNKS
+
+    def piece(ref, chunk):
+        return ref.at[pl.ds(chunk * rows, rows)]
+
+    def copy(src, block, chunk, send, recv, target):
         return pltpu.make_async_remote_copy(
-            src_ref=src,
-            dst_ref=all_ref.at[block],
+            src_ref=piece(src, chunk),
+            dst_ref=piece(all_ref.at[block], chunk),
             send_sem=send,
             recv_sem=recv,
             device_id=(group, lax.div(target, dp_count), lax.rem(target, dp_count)),
@@ -169,32 +175,40 @@
         )
     pl.semaphore_wait(barrier, 3)
 
-    hops = (n // 2, n - 1 - n // 2)
+    hops = [
+        [n // 2 if way == chunk % 2 else n - 1 - n // 2 for way in (0, 1)]
+        for chunk in range(CHUNKS)
+    ]
     ring, pair = {}, []
 
-    def ring_start(way, hop, src, block):
-        k = hop + way * hops[0]
-        ring[way, hop] = copy(src, block, ring_out.at[k], ring_in.at[k], (right, left)[way])
-        ring[way, hop].start()
-
-    def pair_start(src, block):
+    def ring_start(chunk, way, hop, src, block):
+        k = len(ring)
+        ring[chunk, way, hop] = copy(
+            src, block, chunk, ring_out.at[k], ring_in.at[k], (right, left)[way]
+        )
+        ring[chunk, way, hop].start()
+
+    def pair_start(chunk, src, block):
         j = len(pair)
-        pair.append(copy(src, block, pair_out.at[j], pair_in.at[j], other))
+        pair.append(copy(src, block, chunk, pair_out.at[j], pair_in.at[j], other))
         pair[-1].start()
 
-    ring_start(0, 0, own_ref, flat)
-    ring_start(1, 0, own_ref, flat)
+    for chunk in range(CHUNKS):
+        for way in (0, 1):
+            ring_start(chunk, way, 0, own_ref, flat)
     local = pltpu.make_async_copy(own_ref, all_ref.at[flat], local_sem)
     local.start()
-    pair_start(own_ref, flat)
-    for hop in range(hops[0]):
-        for way in (0, 1):
-            if hop < hops[way]:
-                block = at((-1, 1)[way] * (hop + 1))
-                ring[way, hop].wait_recv()
-                if hop + 1 < hops[way]:
-                    ring_start(way, hop + 1, all_ref.at[block], block)
-                pair_start(all_ref.at[block], block)
+    for chunk in range(CHUNKS):
+        pair_start(chunk, own_ref, flat)
+    for hop in range(n // 2):
+        for chunk in range(CHUNKS):
+            for way in (0, 1):
+                if hop < hops[chunk][way]:
+                    block = at((-1, 1)[way] * (hop + 1))
+                    ring[chunk, way, hop].wait_recv()
+                    if hop + 1 < hops[chunk][way]:
+                        ring_start(chunk, way, hop + 1, all_ref.at[block], block)
+                    pair_start(chunk, all_ref.at[block], block)
     for sent in ring.values():
         sent.wait_send()
     for sent in pair:
@@ -211,10 +225,10 @@
         out_specs=pl.BlockSpec(memory_space=pl.ANY),
         scratch_shapes=[
             pltpu.SemaphoreType.DMA,
-            pltpu.SemaphoreType.DMA((n - 1,)),
-            pltpu.SemaphoreType.DMA((n - 1,)),
-            pltpu.SemaphoreType.DMA((n,)),
-            pltpu.SemaphoreType.DMA((n,)),
+            pltpu.SemaphoreType.DMA((CHUNKS * (n - 1),)),
+            pltpu.SemaphoreType.DMA((CHUNKS * (n - 1),)),
+            pltpu.SemaphoreType.DMA((CHUNKS * n,)),
+            pltpu.SemaphoreType.DMA((CHUNKS * n,)),
         ],
         compiler_params=pltpu.CompilerParams(collective_id=0, has_side_effects=True),
     )(block)

time: 189 us -> 182 us (0.963)
  Pallas kernels: 86.1 us -> 80.4 us
    pallas_call x1, Pallas kernels: 48.9 us -> 43 us  [gather_all(): pl.pallas_call(functools.partial(gather_kernel, n, dp_count), out_shape=j...]
  transfers between devices with their start and end apart: 2 -> 2, of which waited for: 2 -> 2; matrix products, arithmetic and copies ran while one was open for 9% -> 10% of each run, Pallas kernels for 20% -> 21%
where the time goes in v4:
time: 182 us; the launch traced here: 181 us
  Pallas kernels  80.4 us (44%)
  waiting for transfers between devices  59.4 us (33%)
  local copies, waits for them, and re-layouts  16.3 us (9%)
  starting transfers between devices  10.5 us (6%)
  matrix products  9.2 us (5%)
  other arithmetic  4.93 us (3%)
    pallas_call x1, Pallas kernels, gather_all(): pl.pallas_call(functools.partial(gather_kernel, n, dp_count), out_shape=j...  43 us
    all_to_all x1, waiting for transfers between devices, per_device(): lax.all_to_all(parts.reshape(slice_count, capacity, features), both, spli...  34.1 us
    all_to_all x1, waiting for transfers between devices, per_device(): lax.all_to_all(fetched, 'expert', split_axis=0, concat_axis=0, tiled=True)  25.3 us
    pallas_call x1, Pallas kernels, expert_mlp(): pl.pallas_call(mlp_kernel, out_shape=jax.ShapeDtypeStruct((rows, features...  19.6 us
    pallas_call x1, Pallas kernels, attend(): pl.pallas_call(attend_kernel, out_shape=jax.ShapeDtypeStruct((requests, n...  17.8 us
    dot_general x1, matrix products, per_device(): jnp.dot(dispatch, gathered.reshape(slice_count * token_rows, -1), preferr...  6.65 us
    all_to_all x1, starting transfers between devices, per_device(): lax.all_to_all(fetched, 'expert', split_axis=0, concat_axis=0, tiled=True)  5.6 us
    all_to_all x1, starting transfers between devices, per_device(): lax.all_to_all(parts.reshape(slice_count, capacity, features), both, spli...  4.91 us
  transfers between devices with their start and end apart: 2, of which 2 were waited for; matrix products, arithmetic and copies ran while one was open for 10% of the time, Pallas kernels for 21%

profile of v4, /device:TPU:15, one launch (start us, length us, event | category | flops | bytes accessed | tf_op | source)
XLA Modules:
  0.0 181.5 jit_solution(12043684648208671412)
XLA Ops:
  0.6 0.8 eq.105
  1.4 0.2 convert_reduce_fusion
  1.7 0.7 broadcast_multiply_fusion
  2.3 0.8 broadcast_in_dim.42
  3.1 0.1 select_reduce_fusion.1
  3.2 0.1 copy.24
  3.3 0.1 reshape.196
  3.4 0.7 convert_element_type.60
  4.1 0.1 copy.25
  4.3 1.8 %fusion.7.own_ref = bf16[64,3712]{1,0:T(8,128)(2,1)} fusion(bf16[64,36]{1,0:T(8,128)(2,1)S(1)} %pad_maximum_fusion, bf16[64,3584]{1,0:T(8,128)(2,1)} %param.18), kind=kLoop, calls=%fused_computation.17 | loop fusion | flops 1425408 | bytes 938496 | tf_op jit(solution)/shard_map/concatenate | solution.py:299
  6.1 43.0 %shard_map.131 = bf16[16,64,3712]{2,1,0:T(8,128)(2,1)} custom-call(bf16[64,3712]{1,0:T(8,128)(2,1)} %fusion.7.own_ref), custom_call_target="tpu_custom_call" | custom-call | tf_op jit(solution)/shard_map/pallas_call | solution.py:221
  49.1 0.8 slice.10
  49.9 0.1 copy.26
  50.1 0.1 reshape.180
  50.4 2.3 %gather_fusion = bf16[32,288,128]{2,1,0:T(8,128)(2,1)} fusion(bf16[8,288,128]{2,1,0:T(8,128)(2,1)S(1)} %bitcast.34, s32[1024]{0:T(1024)S(1)} %get-tuple-element.9), kind=kCustom, calls=%fused_computation | custom fusion | bytes 4718720 | tf_op jit(solution)/shard_map/gather | solution.py:319
  52.7 5.6 %all-to-all-start = ((bf16[16,2,288,128]{3,2,1,0:T(8,128)(2,1)}), bf16[16,2,288,128]{3,2,1,0:T(8,128)(2,1)S(1)}, u32[]{:S(2)}, u32[]{:S(2)}) async-start(bf16[16,2,288,128]{3,2,1,0:T(8,128)(2,1)} %bitcast.4), calls=%async_computation | async-start | bytes 4718592 | tf_op jit(solution)/shard_map/all_to_all | solution.py:320
  58.3 1.3 compare_reduce_fusion
  59.6 0.1 fusion.4
  59.8 6.6 %convolution_convert_fusion.x_ref = bf16[384,3712]{1,0:T(8,128)(2,1)S(1)} fusion(bf16[1024,3712]{1,0:T(8,128)(2,1)} %bitcast.35, s32[1024]{0:T(1024)S(1)} %eq.117), kind=kOutput, calls=%fused_computation.2 | convolution fusion | flops 2921054208 | bytes 10457088 | tf_op jit(solution)/shard_map/dot_general | solution.py:322
  66.4 19.6 %shard_map.132 = bf16[384,3584]{1,0:T(8,128)(2,1)} custom-call(bf16[384,3712]{1,0:T(8,128)(2,1)S(1)} %convolution_convert_fusion.x_ref, bf16[1,3584,1024]{2,1,0:T(8,128)(2,1)} %gate_ref.1, bf16[1,3584,1024]{2,1,0:T(8,128)(2,1)} %up_ref.1, bf16[1,1024,3584]{2,1,0:T(8,128)(2,1)} %down_ref.1), custom_call_target="tpu_custom_call" | custom-call | flops 8455716864 | bytes 27525120 | tf_op jit(solution)/shard_map/pallas_call | solution.py:114
  86.0 25.3 %all-to-all-done = bf16[16,2,288,128]{3,2,1,0:T(8,128)(2,1)S(1)} async-done(((bf16[16,2,288,128]{3,2,1,0:T(8,128)(2,1)}), bf16[16,2,288,128]{3,2,1,0:T(8,128)(2,1)S(1)}, u32[]{:S(2)}, u32[]{:S(2)}) %all-to-all-start) | async-done | bytes 2359328 | tf_op jit(solution)/shard_map/all_to_all | solution.py:320
  111.3 1.4 copy-done.1
  112.7 4.9 %all-to-all-start.1 = ((bf16[16,24,3584]{2,1,0:T(8,128)(2,1)}), bf16[16,24,3584]{2,1,0:T(8,128)(2,1)S(1)}, u32[]{:S(2)}, u32[]{:S(2)}) async-start(bf16[16,24,3584]{2,1,0:T(8,128)(2,1)} %bitcast.10), calls=%async_computation.1 | async-start | bytes 5505024 | tf_op jit(solution)/shard_map/all_to_all | solution.py:327
  117.6 0.1 reshape.172
  117.8 0.1 fusion.2
  117.9 3.5 %gather_fusion.1 = bf16[16,288,128]{2,1,0:T(8,128)(2,1)} fusion(bf16[32,288,128]{2,1,0:T(8,128)(2,1)} %bitcast.36, s32[1024]{0:T(1024)S(1)} %get-tuple-element.8), kind=kCustom, calls=%fused_computation.1 | custom fusion | bytes 2359360 | tf_op jit(solution)/shard_map/gather | solution.py:335
  121.4 3.5 %reshape.171 = bf16[2,512,576]{2,1,0:T(8,128)(2,1)} reshape(bf16[16,288,128]{2,1,0:T(8,128)(2,1)} %gather_fusion.1) | data formatting | bytes 2359296 | tf_op jit(solution)/shard_map/reshape | solution.py:336
  124.9 1.4 constant_dynamic-update-slice_fusion.1
  126.3 0.9 fusion.18
  127.2 17.8 %shard_map.133 = bf16[2,32,32768]{2,1,0:T(8,128)(2,1)} custom-call(s32[2]{0:T(128)S(1)} %copy-done, bf16[2,32,36864]{2,1,0:T(8,128)(2,1)} %q_ref.1, bf16[2,544,640]{2,1,0:T(8,128)(2,1)S(1)} %get-tuple-element.7.even_ref, bf16[2,544,640]{2,1,0:T(8,128)(2,1)S(1)} %get-tuple-element.6.odd_ref), custom_call_target="tpu_custom_call" | custom-call | flops 4848615424 | bytes 8912896 | tf_op jit(solution)/shard_map/pallas_call | solution.py:62
  145.0 34.1 %all-to-all-done.1 = bf16[16,24,3584]{2,1,0:T(8,128)(2,1)S(1)} async-done(((bf16[16,24,3584]{2,1,0:T(8,128)(2,1)}), bf16[16,24,3584]{2,1,0:T(8,128)(2,1)S(1)}, u32[]{:S(2)}, u32[]{:S(2)}) %all-to-all-start.1) | async-done | bytes 2752544 | tf_op jit(solution)/shard_map/all_to_all | solution.py:327
  179.1 2.4 %fusion = bf16[64,3584]{1,0:T(8,128)(2,1)} fusion(bf16[16,24,3584]{2,1,0:T(8,128)(2,1)S(1)} %all-to-all-done.1, f32[16,64]{1,0:T(8,128)S(1)} %bitcast.38, s32[16,24]{1,0:T(8,128)S(1)} %multiply_add_fusion, s32[16,64]{1,0:T(8,128)S(1)} %fusion.2), kind=kOutput, calls=%fused_computation.4 | convolution fusion | flops 1057243136 | bytes 3220992 | tf_op jit(solution)/shard_map/dot_general | solution.py:354
  (30 shorter events, 0.7 us)
Async XLA Ops:
  6.1 44.2 %copy-start.2 = (bf16[8,36864]{1,0:T(8,128)(2,1)S(1)}, bf16[8,36864]{1,0:T(8,128)(2,1)}, u32[]{:S(2)}) copy-start(bf16[8,36864]{1,0:T(8,128)(2,1)} %param.12) | copy-start | bytes 1769476
  52.7 58.6 %all-to-all-start = ((bf16[16,2,288,128]{3,2,1,0:T(8,128)(2,1)}), bf16[16,2,288,128]{3,2,1,0:T(8,128)(2,1)S(1)}, u32[]{:S(2)}, u32[]{:S(2)}) async-start(bf16[16,2,288,128]{3,2,1,0:T(8,128)(2,1)} %bitcast.4), calls=%async_computation | async-start | bytes 4718592 | tf_op jit(solution)/shard_map/all_to_all | solution.py:320
  111.3 1.4 copy-start.1
  111.3 6.3 %copy-start.3 = (bf16[2,18432]{1,0:T(2,128)(2,1)S(1)}, bf16[2,18432]{1,0:T(2,128)(2,1)}, u32[]{:S(2)}) copy-start(bf16[2,18432]{1,0:T(2,128)(2,1)} %param.17) | copy-start | bytes 221188
  111.3 6.5 %copy-start.4 = (s32[64,4]{0,1:T(4,128)S(1)}, s32[64,4]{0,1:T(4,128)}, u32[]{:S(2)}) copy-start(s32[64,4]{0,1:T(4,128)} %param.19) | copy-start | bytes 3076
  111.3 6.5 %copy-start.5 = (f32[64,4]{0,1:T(4,128)S(1)}, f32[64,4]{0,1:T(4,128)}, u32[]{:S(2)}) copy-start(f32[64,4]{0,1:T(4,128)} %param.20) | copy-start | bytes 3076
  112.7 66.4 %all-to-all-start.1 = ((bf16[16,24,3584]{2,1,0:T(8,128)(2,1)}), bf16[16,24,3584]{2,1,0:T(8,128)(2,1)S(1)}, u32[]{:S(2)}, u32[]{:S(2)}) async-start(bf16[16,24,3584]{2,1,0:T(8,128)(2,1)} %bitcast.10), calls=%async_computation.1 | async-start | bytes 5505024 | tf_op jit(solution)/shard_map/all_to_all | solution.py:327
  126.3 0.9 copy-start

commit v5 on v4

--- a/solution.py
+++ b/solution.py
@@ -13,7 +13,7 @@
 EXPERTS = 16
 CAPP = 2
 ASK_LANES = 128
-CHUNKS = 2
+CHUNK_ROWS = 16
 WINDOW = 640
 LOG2E = 1.4426950408889634
 SCALE = 192.0 ** (-0.5)
@@ -149,7 +149,8 @@
             q = 2 * (q + down * (n - 1 - 2 * q)) + down
         return 2 * q + core
 
-    rows = own_ref.shape[0] // CHUNKS
+    rows = CHUNK_ROWS
+    chunks = own_ref.shape[0] // rows
 
     def piece(ref, chunk):
         return ref.at[pl.ds(chunk * rows, rows)]
@@ -177,7 +178,7 @@
 
     hops = [
         [n // 2 if way == chunk % 2 else n - 1 - n // 2 for way in (0, 1)]
-        for chunk in range(CHUNKS)
+        for chunk in range(chunks)
     ]
     ring, pair = {}, []
 
@@ -193,15 +194,15 @@
         pair.append(copy(src, block, chunk, pair_out.at[j], pair_in.at[j], other))
         pair[-1].start()
 
-    for chunk in range(CHUNKS):
+    for chunk in range(chunks):
         for way in (0, 1):
             ring_start(chunk, way, 0, own_ref, flat)
     local = pltpu.make_async_copy(own_ref, all_ref.at[flat], local_sem)
     local.start()
-    for chunk in range(CHUNKS):
+    for chunk in range(chunks):
         pair_start(chunk, own_ref, flat)
     for hop in range(n // 2):
-        for chunk in range(CHUNKS):
+        for chunk in range(chunks):
             for way in (0, 1):
                 if hop < hops[chunk][way]:
                     block = at((-1, 1)[way] * (hop + 1))
@@ -218,6 +219,7 @@
 
 def gather_all(block, dp_count, count):
     n = count // 2
+    chunks = block.shape[0] // CHUNK_ROWS
     return pl.pallas_call(
         functools.partial(gather_kernel, n, dp_count),
         out_shape=jax.ShapeDtypeStruct((count,) + block.shape, block.dtype),
@@ -225,10 +227,10 @@
         out_specs=pl.BlockSpec(memory_space=pl.ANY),
         scratch_shapes=[
             pltpu.SemaphoreType.DMA,
-            pltpu.SemaphoreType.DMA((CHUNKS * (n - 1),)),
-            pltpu.SemaphoreType.DMA((CHUNKS * (n - 1),)),
-            pltpu.SemaphoreType.DMA((CHUNKS * n,)),
-            pltpu.SemaphoreType.DMA((CHUNKS * n,)),
+            pltpu.SemaphoreType.DMA((chunks * (n - 1),)),
+            pltpu.SemaphoreType.DMA((chunks * (n - 1),)),
+            pltpu.SemaphoreType.DMA((chunks * n,)),
+            pltpu.SemaphoreType.DMA((chunks * n,)),
         ],
         compiler_params=pltpu.CompilerParams(collective_id=0, has_side_effects=True),
     )(block)

time: 182 us -> 181 us (level)
  no operation moved by 1% of the time
where the time goes in v5:
time: 181 us; the launch traced here: 180 us
  Pallas kernels  79.8 us (44%)
  waiting for transfers between devices  59.5 us (33%)
  local copies, waits for them, and re-layouts  16.3 us (9%)
  starting transfers between devices  9.82 us (5%)
  matrix products  9.2 us (5%)
  other arithmetic  4.93 us (3%)
    pallas_call x1, Pallas kernels, gather_all(): pl.pallas_call(functools.partial(gather_kernel, n, dp_count), out_shape=j...  42.6 us
    all_to_all x1, waiting for transfers between devices, per_device(): lax.all_to_all(parts.reshape(slice_count, capacity, features), both, spli...  34.1 us
    all_to_all x1, waiting for transfers between devices, per_device(): lax.all_to_all(fetched, 'expert', split_axis=0, concat_axis=0, tiled=True)  25.4 us
    pallas_call x1, Pallas kernels, expert_mlp(): pl.pallas_call(mlp_kernel, out_shape=jax.ShapeDtypeStruct((rows, features...  19.5 us
    pallas_call x1, Pallas kernels, attend(): pl.pallas_call(attend_kernel, out_shape=jax.ShapeDtypeStruct((requests, n...  17.8 us
    dot_general x1, matrix products, per_device(): jnp.dot(dispatch, gathered.reshape(slice_count * token_rows, -1), preferr...  6.65 us
    all_to_all x1, starting transfers between devices, per_device(): lax.all_to_all(fetched, 'expert', split_axis=0, concat_axis=0, tiled=True)  4.91 us
    all_to_all x1, starting transfers between devices, per_device(): lax.all_to_all(parts.reshape(slice_count, capacity, features), both, spli...  4.91 us
  transfers between devices with their start and end apart: 2, of which 2 were waited for; matrix products, arithmetic and copies ran while one was open for 10% of the time, Pallas kernels for 21%

profile of v5, /device:TPU:15, one launch (start us, length us, event | category | flops | bytes accessed | tf_op | source)
XLA Modules:
  0.0 180.4 jit_solution(1634075921307223275)
XLA Ops:
  0.6 0.8 eq.105
  1.4 0.2 convert_reduce_fusion
  1.7 0.7 broadcast_multiply_fusion
  2.3 0.8 broadcast_in_dim.42
  3.1 0.1 select_reduce_fusion.1
  3.2 0.1 copy.24
  3.3 0.1 reshape.196
  3.4 0.7 convert_element_type.60
  4.1 0.1 copy.25
  4.3 1.8 %fusion.7.own_ref = bf16[64,3712]{1,0:T(8,128)(2,1)} fusion(bf16[64,36]{1,0:T(8,128)(2,1)S(1)} %pad_maximum_fusion, bf16[64,3584]{1,0:T(8,128)(2,1)} %param.18), kind=kLoop, calls=%fused_computation.17 | loop fusion | flops 1425408 | bytes 938496 | tf_op jit(solution)/shard_map/concatenate | solution.py:301
  6.1 42.6 %shard_map.131 = bf16[16,64,3712]{2,1,0:T(8,128)(2,1)} custom-call(bf16[64,3712]{1,0:T(8,128)(2,1)} %fusion.7.own_ref), custom_call_target="tpu_custom_call" | custom-call | tf_op jit(solution)/shard_map/pallas_call | solution.py:223
  48.7 0.8 slice.10
  49.6 0.1 copy.26
  49.8 0.1 reshape.180
  50.1 2.3 %gather_fusion = bf16[32,288,128]{2,1,0:T(8,128)(2,1)} fusion(bf16[8,288,128]{2,1,0:T(8,128)(2,1)S(1)} %bitcast.34, s32[1024]{0:T(1024)S(1)} %get-tuple-element.9), kind=kCustom, calls=%fused_computation | custom fusion | bytes 4718720 | tf_op jit(solution)/shard_map/gather | solution.py:321
  52.3 4.9 %all-to-all-start = ((bf16[16,2,288,128]{3,2,1,0:T(8,128)(2,1)}), bf16[16,2,288,128]{3,2,1,0:T(8,128)(2,1)S(1)}, u32[]{:S(2)}, u32[]{:S(2)}) async-start(bf16[16,2,288,128]{3,2,1,0:T(8,128)(2,1)} %bitcast.4), calls=%async_computation | async-start | bytes 4718592 | tf_op jit(solution)/shard_map/all_to_all | solution.py:322
  57.2 1.3 compare_reduce_fusion
  58.5 0.1 fusion.4
  58.7 6.6 %convolution_convert_fusion.x_ref = bf16[384,3712]{1,0:T(8,128)(2,1)S(1)} fusion(bf16[1024,3712]{1,0:T(8,128)(2,1)} %bitcast.35, s32[1024]{0:T(1024)S(1)} %eq.117), kind=kOutput, calls=%fused_computation.2 | convolution fusion | flops 2921054208 | bytes 10457088 | tf_op jit(solution)/shard_map/dot_general | solution.py:324
  65.3 19.5 %shard_map.132 = bf16[384,3584]{1,0:T(8,128)(2,1)} custom-call(bf16[384,3712]{1,0:T(8,128)(2,1)S(1)} %convolution_convert_fusion.x_ref, bf16[1,3584,1024]{2,1,0:T(8,128)(2,1)} %gate_ref.1, bf16[1,3584,1024]{2,1,0:T(8,128)(2,1)} %up_ref.1, bf16[1,1024,3584]{2,1,0:T(8,128)(2,1)} %down_ref.1), custom_call_target="tpu_custom_call" | custom-call | flops 8455716864 | bytes 27525120 | tf_op jit(solution)/shard_map/pallas_call | solution.py:114
  84.8 25.4 %all-to-all-done = bf16[16,2,288,128]{3,2,1,0:T(8,128)(2,1)S(1)} async-done(((bf16[16,2,288,128]{3,2,1,0:T(8,128)(2,1)}), bf16[16,2,288,128]{3,2,1,0:T(8,128)(2,1)S(1)}, u32[]{:S(2)}, u32[]{:S(2)}) %all-to-all-start) | async-done | bytes 2359328 | tf_op jit(solution)/shard_map/all_to_all | solution.py:322
  110.3 1.4 copy-done.1
  111.7 4.9 %all-to-all-start.1 = ((bf16[16,24,3584]{2,1,0:T(8,128)(2,1)}), bf16[16,24,3584]{2,1,0:T(8,128)(2,1)S(1)}, u32[]{:S(2)}, u32[]{:S(2)}) async-start(bf16[16,24,3584]{2,1,0:T(8,128)(2,1)} %bitcast.10), calls=%async_computation.1 | async-start | bytes 5505024 | tf_op jit(solution)/shard_map/all_to_all | solution.py:329
  116.6 0.1 reshape.172
  116.8 0.1 fusion.2
  116.9 3.5 %gather_fusion.1 = bf16[16,288,128]{2,1,0:T(8,128)(2,1)} fusion(bf16[32,288,128]{2,1,0:T(8,128)(2,1)} %bitcast.36, s32[1024]{0:T(1024)S(1)} %get-tuple-element.8), kind=kCustom, calls=%fused_computation.1 | custom fusion | bytes 2359360 | tf_op jit(solution)/shard_map/gather | solution.py:337
  120.3 3.5 %reshape.171 = bf16[2,512,576]{2,1,0:T(8,128)(2,1)} reshape(bf16[16,288,128]{2,1,0:T(8,128)(2,1)} %gather_fusion.1) | data formatting | bytes 2359296 | tf_op jit(solution)/shard_map/reshape | solution.py:338
  123.8 1.4 constant_dynamic-update-slice_fusion.1
  125.3 0.9 fusion.18
  126.2 17.8 %shard_map.133 = bf16[2,32,32768]{2,1,0:T(8,128)(2,1)} custom-call(s32[2]{0:T(128)S(1)} %copy-done, bf16[2,32,36864]{2,1,0:T(8,128)(2,1)} %q_ref.1, bf16[2,544,640]{2,1,0:T(8,128)(2,1)S(1)} %get-tuple-element.7.even_ref, bf16[2,544,640]{2,1,0:T(8,128)(2,1)S(1)} %get-tuple-element.6.odd_ref), custom_call_target="tpu_custom_call" | custom-call | flops 4848615424 | bytes 8912896 | tf_op jit(solution)/shard_map/pallas_call | solution.py:62
  144.0 34.1 %all-to-all-done.1 = bf16[16,24,3584]{2,1,0:T(8,128)(2,1)S(1)} async-done(((bf16[16,24,3584]{2,1,0:T(8,128)(2,1)}), bf16[16,24,3584]{2,1,0:T(8,128)(2,1)S(1)}, u32[]{:S(2)}, u32[]{:S(2)}) %all-to-all-start.1) | async-done | bytes 2752544 | tf_op jit(solution)/shard_map/all_to_all | solution.py:329
  178.0 2.4 %fusion = bf16[64,3584]{1,0:T(8,128)(2,1)} fusion(bf16[16,24,3584]{2,1,0:T(8,128)(2,1)S(1)} %all-to-all-done.1, f32[16,64]{1,0:T(8,128)S(1)} %bitcast.38, s32[16,24]{1,0:T(8,128)S(1)} %multiply_add_fusion, s32[16,64]{1,0:T(8,128)S(1)} %fusion.2), kind=kOutput, calls=%fused_computation.4 | convolution fusion | flops 1057243136 | bytes 3220992 | tf_op jit(solution)/shard_map/dot_general | solution.py:356
  (30 shorter events, 0.7 us)
Async XLA Ops:
  6.1 43.8 %copy-start.2 = (bf16[8,36864]{1,0:T(8,128)(2,1)S(1)}, bf16[8,36864]{1,0:T(8,128)(2,1)}, u32[]{:S(2)}) copy-start(bf16[8,36864]{1,0:T(8,128)(2,1)} %param.12) | copy-start | bytes 1769476
  52.3 57.9 %all-to-all-start = ((bf16[16,2,288,128]{3,2,1,0:T(8,128)(2,1)}), bf16[16,2,288,128]{3,2,1,0:T(8,128)(2,1)S(1)}, u32[]{:S(2)}, u32[]{:S(2)}) async-start(bf16[16,2,288,128]{3,2,1,0:T(8,128)(2,1)} %bitcast.4), calls=%async_computation | async-start | bytes 4718592 | tf_op jit(solution)/shard_map/all_to_all | solution.py:322
  110.3 1.4 copy-start.1
  110.3 6.3 %copy-start.3 = (bf16[2,18432]{1,0:T(2,128)(2,1)S(1)}, bf16[2,18432]{1,0:T(2,128)(2,1)}, u32[]{:S(2)}) copy-start(bf16[2,18432]{1,0:T(2,128)(2,1)} %param.17) | copy-start | bytes 221188
  110.3 6.5 %copy-start.4 = (s32[64,4]{0,1:T(4,128)S(1)}, s32[64,4]{0,1:T(4,128)}, u32[]{:S(2)}) copy-start(s32[64,4]{0,1:T(4,128)} %param.19) | copy-start | bytes 3076
  110.3 6.5 %copy-start.5 = (f32[64,4]{0,1:T(4,128)S(1)}, f32[64,4]{0,1:T(4,128)}, u32[]{:S(2)}) copy-start(f32[64,4]{0,1:T(4,128)} %param.20) | copy-start | bytes 3076
  111.7 66.4 %all-to-all-start.1 = ((bf16[16,24,3584]{2,1,0:T(8,128)(2,1)}), bf16[16,24,3584]{2,1,0:T(8,128)(2,1)S(1)}, u32[]{:S(2)}, u32[]{:S(2)}) async-start(bf16[16,24,3584]{2,1,0:T(8,128)(2,1)} %bitcast.10), calls=%async_computation.1 | async-start | bytes 5505024 | tf_op jit(solution)/shard_map/all_to_all | solution.py:329
  125.2 0.9 copy-start

commit v6 on v5

--- a/solution.py
+++ b/solution.py
@@ -325,7 +325,6 @@
         dispatch, gathered.reshape(slice_count * token_rows, -1), preferred_element_type=jnp.float32
     ).astype(jnp.bfloat16)
     parts = expert_mlp(received, w_gate, w_up, w_down)
-    parts, arrived = lax.optimization_barrier((parts, arrived))
     returned = lax.all_to_all(
         parts.reshape(slice_count, capacity, features), both, split_axis=0, concat_axis=0, tiled=True
     )

time: 181 us -> 180 us (level)
  no operation moved by 1% of the time
where the time goes in v6:
time: 180 us
  Pallas kernels  80 us (44%)
  waiting for transfers between devices  59.2 us (33%)
  local copies, waits for them, and re-layouts  16.3 us (9%)
  starting transfers between devices  9.82 us (5%)
  matrix products  9.2 us (5%)
  other arithmetic  4.26 us (2%)
    pallas_call x1, Pallas kernels, gather_all(): pl.pallas_call(functools.partial(gather_kernel, n, dp_count), out_shape=j...  42.6 us
    all_to_all x1, waiting for transfers between devices, per_device(): lax.all_to_all(parts.reshape(slice_count, capacity, features), both, spli...  33.9 us
    all_to_all x1, waiting for transfers between devices, per_device(): lax.all_to_all(fetched, 'expert', split_axis=0, concat_axis=0, tiled=True)  25.3 us
    pallas_call x1, Pallas kernels, expert_mlp(): pl.pallas_call(mlp_kernel, out_shape=jax.ShapeDtypeStruct((rows, features...  19.6 us
    pallas_call x1, Pallas kernels, attend(): pl.pallas_call(attend_kernel, out_shape=jax.ShapeDtypeStruct((requests, n...  17.8 us
    dot_general x1, matrix products, per_device(): jnp.dot(dispatch, gathered.reshape(slice_count * token_rows, -1), preferr...  6.65 us
    all_to_all x1, starting transfers between devices, per_device(): lax.all_to_all(fetched, 'expert', split_axis=0, concat_axis=0, tiled=True)  4.91 us
    all_to_all x1, starting transfers between devices, per_device(): lax.all_to_all(parts.reshape(slice_count, capacity, features), both, spli...  4.91 us
  transfers between devices with their start and end apart: 2, of which 2 were waited for; matrix products, arithmetic and copies ran while one was open for 10% of the time, Pallas kernels for 21%

profile of v6, /device:TPU:15, one launch (start us, length us, event | category | flops | bytes accessed | tf_op | source)
XLA Modules:
  0.0 179.6 jit_solution(819733734468280769)
XLA Ops:
  0.6 0.8 eq.104
  1.4 0.2 convert_reduce_fusion
  1.7 0.8 broadcast_in_dim.42
  2.4 0.1 select_reduce_fusion.1
  2.5 0.1 copy.24
  2.6 0.1 reshape.196
  2.7 0.7 convert_element_type.60
  3.4 0.1 copy.25
  3.6 1.8 %fusion.7.own_ref = bf16[64,3712]{1,0:T(8,128)(2,1)} fusion(bf16[64,36]{1,0:T(8,128)(2,1)S(1)} %pad_maximum_fusion, bf16[64,3584]{1,0:T(8,128)(2,1)} %param.18), kind=kLoop, calls=%fused_computation.17 | loop fusion | flops 1425408 | bytes 938496 | tf_op jit(solution)/shard_map/concatenate | solution.py:301
  5.4 42.6 %shard_map.131 = bf16[16,64,3712]{2,1,0:T(8,128)(2,1)} custom-call(bf16[64,3712]{1,0:T(8,128)(2,1)} %fusion.7.own_ref), custom_call_target="tpu_custom_call" | custom-call | tf_op jit(solution)/shard_map/pallas_call | solution.py:223
  48.0 0.8 slice.9
  48.9 0.1 copy.26
  49.0 0.1 copy.27
  49.1 0.1 reshape.180
  49.3 2.3 %gather_fusion = bf16[32,288,128]{2,1,0:T(8,128)(2,1)} fusion(bf16[8,288,128]{2,1,0:T(8,128)(2,1)S(1)} %bitcast.34, s32[1024]{0:T(1024)S(1)} %pad_clamp_fusion.1), kind=kCustom, calls=%fused_computation | custom fusion | bytes 4718720 | tf_op jit(solution)/shard_map/gather | solution.py:321
  51.5 4.9 %all-to-all-start = ((bf16[16,2,288,128]{3,2,1,0:T(8,128)(2,1)}), bf16[16,2,288,128]{3,2,1,0:T(8,128)(2,1)S(1)}, u32[]{:S(2)}, u32[]{:S(2)}) async-start(bf16[16,2,288,128]{3,2,1,0:T(8,128)(2,1)} %bitcast.3), calls=%async_computation | async-start | bytes 4718592 | tf_op jit(solution)/shard_map/all_to_all | solution.py:322
  56.5 1.3 compare_reduce_fusion
  57.8 0.1 fusion.2
  57.9 6.6 %convolution_convert_fusion.x_ref = bf16[384,3712]{1,0:T(8,128)(2,1)S(1)} fusion(bf16[1024,3712]{1,0:T(8,128)(2,1)} %bitcast.35, s32[1024]{0:T(1024)S(1)} %eq.123), kind=kOutput, calls=%fused_computation.2 | convolution fusion | flops 2921054208 | bytes 10457088 | tf_op jit(solution)/shard_map/dot_general | solution.py:324
  64.6 19.6 %shard_map.133 = bf16[384,3584]{1,0:T(8,128)(2,1)} custom-call(bf16[384,3712]{1,0:T(8,128)(2,1)S(1)} %convolution_convert_fusion.x_ref, bf16[1,3584,1024]{2,1,0:T(8,128)(2,1)} %gate_ref.1, bf16[1,3584,1024]{2,1,0:T(8,128)(2,1)} %up_ref.1, bf16[1,1024,3584]{2,1,0:T(8,128)(2,1)} %down_ref.1), custom_call_target="tpu_custom_call" | custom-call | flops 8455716864 | bytes 27525120 | tf_op jit(solution)/shard_map/pallas_call | solution.py:114
  84.2 25.3 %all-to-all-done = bf16[16,2,288,128]{3,2,1,0:T(8,128)(2,1)S(1)} async-done(((bf16[16,2,288,128]{3,2,1,0:T(8,128)(2,1)}), bf16[16,2,288,128]{3,2,1,0:T(8,128)(2,1)S(1)}, u32[]{:S(2)}, u32[]{:S(2)}) %all-to-all-start) | async-done | bytes 2359328 | tf_op jit(solution)/shard_map/all_to_all | solution.py:322
  109.5 1.4 copy-done.1
  110.9 4.9 %all-to-all-start.1 = ((bf16[16,24,3584]{2,1,0:T(8,128)(2,1)}), bf16[16,24,3584]{2,1,0:T(8,128)(2,1)S(1)}, u32[]{:S(2)}, u32[]{:S(2)}) async-start(bf16[16,24,3584]{2,1,0:T(8,128)(2,1)} %bitcast.10), calls=%async_computation.1 | async-start | bytes 5505024 | tf_op jit(solution)/shard_map/all_to_all | solution.py:328
  115.9 0.1 reshape.171
  116.1 0.1 fusion.4
  116.2 3.5 %gather_fusion.1 = bf16[16,288,128]{2,1,0:T(8,128)(2,1)} fusion(bf16[32,288,128]{2,1,0:T(8,128)(2,1)} %bitcast.36, s32[1024]{0:T(1024)S(1)} %pad_clamp_fusion), kind=kCustom, calls=%fused_computation.1 | custom fusion | bytes 2359360 | tf_op jit(solution)/shard_map/gather | solution.py:336
  119.7 3.5 %reshape.170 = bf16[2,512,576]{2,1,0:T(8,128)(2,1)} reshape(bf16[16,288,128]{2,1,0:T(8,128)(2,1)} %gather_fusion.1) | data formatting | bytes 2359296 | tf_op jit(solution)/shard_map/reshape | solution.py:337
  123.2 1.4 constant_dynamic-update-slice_fusion.1
  124.6 0.9 fusion.18
  125.5 17.8 %shard_map.132 = bf16[2,32,32768]{2,1,0:T(8,128)(2,1)} custom-call(s32[2]{0:T(128)S(1)} %copy-done, bf16[2,32,36864]{2,1,0:T(8,128)(2,1)} %q_ref.1, bf16[2,544,640]{2,1,0:T(8,128)(2,1)S(1)} %get-tuple-element.3.even_ref, bf16[2,544,640]{2,1,0:T(8,128)(2,1)S(1)} %get-tuple-element.2.odd_ref), custom_call_target="tpu_custom_call" | custom-call | flops 4848615424 | bytes 8912896 | tf_op jit(solution)/shard_map/pallas_call | solution.py:62
  143.3 33.9 %all-to-all-done.1 = bf16[16,24,3584]{2,1,0:T(8,128)(2,1)S(1)} async-done(((bf16[16,24,3584]{2,1,0:T(8,128)(2,1)}), bf16[16,24,3584]{2,1,0:T(8,128)(2,1)S(1)}, u32[]{:S(2)}, u32[]{:S(2)}) %all-to-all-start.1) | async-done | bytes 2752544 | tf_op jit(solution)/shard_map/all_to_all | solution.py:328
  177.3 2.4 %fusion = bf16[64,3584]{1,0:T(8,128)(2,1)} fusion(bf16[16,24,3584]{2,1,0:T(8,128)(2,1)S(1)} %all-to-all-done.1, f32[16,64]{1,0:T(8,128)S(1)} %bitcast.38, s32[16,24]{1,0:T(8,128)S(1)} %multiply_add_fusion, s32[16,64]{1,0:T(8,128)S(1)} %fusion.4), kind=kOutput, calls=%fused_computation.4 | convolution fusion | flops 1057243136 | bytes 3220992 | tf_op jit(solution)/shard_map/dot_general | solution.py:355
  (33 shorter events, 0.6 us)
Async XLA Ops:
  5.4 43.8 %copy-start.2 = (bf16[8,36864]{1,0:T(8,128)(2,1)S(1)}, bf16[8,36864]{1,0:T(8,128)(2,1)}, u32[]{:S(2)}) copy-start(bf16[8,36864]{1,0:T(8,128)(2,1)} %param.12) | copy-start | bytes 1769476
  51.5 57.9 %all-to-all-start = ((bf16[16,2,288,128]{3,2,1,0:T(8,128)(2,1)}), bf16[16,2,288,128]{3,2,1,0:T(8,128)(2,1)S(1)}, u32[]{:S(2)}, u32[]{:S(2)}) async-start(bf16[16,2,288,128]{3,2,1,0:T(8,128)(2,1)} %bitcast.3), calls=%async_computation | async-start | bytes 4718592 | tf_op jit(solution)/shard_map/all_to_all | solution.py:322
  109.5 1.4 copy-start.1
  109.5 6.3 %copy-start.6 = (s32[2,8]{1,0:T(2,128)S(1)}, s32[2,8]{1,0:T(2,128)}, u32[]{:S(2)}) copy-start(s32[2,8]{1,0:T(2,128)} %param.13) | copy-start | bytes 196
  109.5 6.4 %copy-start.3 = (bf16[2,18432]{1,0:T(2,128)(2,1)S(1)}, bf16[2,18432]{1,0:T(2,128)(2,1)}, u32[]{:S(2)}) copy-start(bf16[2,18432]{1,0:T(2,128)(2,1)} %param.17) | copy-start | bytes 221188
  109.5 6.6 %copy-start.4 = (s32[64,4]{0,1:T(4,128)S(1)}, s32[64,4]{0,1:T(4,128)}, u32[]{:S(2)}) copy-start(s32[64,4]{0,1:T(4,128)} %param.19) | copy-start | bytes 3076
  109.5 6.6 %copy-start.5 = (f32[64,4]{0,1:T(4,128)S(1)}, f32[64,4]{0,1:T(4,128)}, u32[]{:S(2)}) copy-start(f32[64,4]{0,1:T(4,128)} %param.20) | copy-start | bytes 3076
  110.9 66.4 %all-to-all-start.1 = ((bf16[16,24,3584]{2,1,0:T(8,128)(2,1)}), bf16[16,24,3584]{2,1,0:T(8,128)(2,1)S(1)}, u32[]{:S(2)}, u32[]{:S(2)}) async-start(bf16[16,24,3584]{2,1,0:T(8,128)(2,1)} %bitcast.10), calls=%async_computation.1 | async-start | bytes 5505024 | tf_op jit(solution)/shard_map/all_to_all | solution.py:328
  124.6 0.9 copy-start
